TPU v7x, 256 devices: a whole 4x4x8 slice. The times are simulated.
256 devices in a mesh: bucket: 16 (over z, core), replica: 16 (over y, x).
Axes of the slice: x: 4, y: 4, z: 8, core: 2. Of those that a mesh axis runs over, the one named last changes fastest.
Arguments:
- rows: bfloat16 [262144, 768], P(('bucket', 'replica')), may hold values from -40 to 40, as said below
- cell_ids: int32 [262144, 1], P(('bucket', 'replica')), may hold values from 0 to 15; in each aligned block of 1024 rows (0 to 1023, 1024 to 2047, ...) at most 128 rows name the same one
- start_basis: float32 [16, 768, 768], P('bucket'), may hold values from -0.1 to 1.1, as said below
Outputs:
- rotated: bfloat16 [262144, 768], P(('bucket', 'replica'))
Inputs may be any that keep to these rules, and one draw needn't show every extreme that they name: `cell_ids`: in the rows of one device no cell is named by more than 128 rows, a bound that some block reaches; every cell is named by some row. `rows`: A residual row: a column offset plus rough noise with column and row scales. `start_basis`: the identity plus small dense entries.
All inputs are finite; a program needn't handle non-finite values.
Results may differ from a plain program's by a relative error of at most 0.0049.
Values may be sent and summed in bfloat16 or wider, within the bound.
A program may use at most 128 MiB of HBM per device.

v0:
```python
import jax
import jax.numpy as jnp
from jax import lax
from jax.sharding import PartitionSpec as P

CELLS = 16
ITERS_NS = 3
CAP = 128


def cell_solve(factor, image):
    return jax.scipy.linalg.solve_triangular(factor, image.T, lower=True).T


def local_gram(image):
    return jnp.einsum("cji,cjk->cik", image, image, precision=lax.Precision.HIGHEST)


def orthonormal(image, gram_matrix):
    factor = jax.vmap(jnp.linalg.cholesky)(gram_matrix)
    return jax.vmap(cell_solve)(factor, image)


def body(rows, cell_ids, start_basis):
    width = rows.shape[1]
    flat_ids = cell_ids[:, 0]
    onehot = (flat_ids[:, None] == jnp.arange(CELLS, dtype=jnp.int32)[None, :]).astype(jnp.int32)
    slot = jnp.sum(jnp.cumsum(onehot, axis=0) * onehot, axis=1) - 1
    send_counts = jnp.sum(onehot, axis=0).astype(jnp.bfloat16)[:, None]
    buffer = jnp.zeros((CELLS, CAP, width), jnp.bfloat16).at[flat_ids, slot].set(rows)
    received, recv_counts = (
        lax.all_to_all(buffer, "bucket", split_axis=0, concat_axis=1, tiled=True),
        lax.all_to_all(send_counts, "bucket", split_axis=0, concat_axis=1, tiled=True),
    )
    count_part = jnp.sum(recv_counts.astype(jnp.float32), axis=1)
    sum_part = jnp.sum(received, axis=1, dtype=jnp.float32)
    square_part = jnp.einsum("crd,cre->cde", received, received, preferred_element_type=jnp.float32)
    count_all, sum_all, square_all = lax.psum((count_part, sum_part, square_part), "replica")
    divisor = jnp.maximum(count_all, 1.0)
    mean = sum_all / divisor[:, None]
    covariance = square_all / divisor[:, None, None] - mean[:, :, None] * mean[:, None, :]
    current = start_basis
    for step in range(ITERS_NS):
        image = jnp.einsum("cij,cjk->cik", covariance, current, precision=lax.Precision.HIGHEST)
        current = orthonormal(image, local_gram(image))
    rotation = current.astype(jnp.bfloat16)
    shift = jnp.einsum(
        "cd,cde->ce", mean, rotation.astype(jnp.float32), precision=lax.Precision.HIGHEST
    )
    product = jnp.einsum("crd,cde->cre", received, rotation, preferred_element_type=jnp.float32)
    rotated_slots = (product - shift[:, None, :]).astype(jnp.bfloat16)
    returned = lax.all_to_all(rotated_slots, "bucket", split_axis=1, concat_axis=0, tiled=True)
    return returned[flat_ids, slot]


def solution(mesh):
    placed = (
        P(("bucket", "replica"), None),
        P(("bucket", "replica"), None),
        P("bucket", None, None),
    )
    return jax.shard_map(
        body, mesh=mesh, in_specs=placed, out_specs=P(("bucket", "replica"), None), check_vma=False
    )
```

profile of v0, /device:TPU:26, one launch (start us, length us, event | category | flops | bytes accessed | tf_op | source)
XLA Modules:
  0.0 1186.5 jit_solution(7130248097209281491)
XLA Ops:
  7.4 4.5 reduce-window.6
  15.3 7.9 scatter_custom_fusion
  23.2 80.8 %all_to_all.31 = bf16[16,128,768]{2,1,0:T(8,128)(2,1)S(1)} all-to-all(bf16[16,128,768]{2,1,0:T(8,128)(2,1)} %bitcast.878), channel_id=1, replica_groups=mesh['bucket'=16,'replica'=16] {'bucket'}, dimensions={0} | all-to-all | bytes 6291456 | tf_op jit(solution)/shard_map/all_to_all | solution.py:32
  105.7 4.1 convolution_bitcast_fusion
  110.5 4.2 all-to-all-start.1
  114.7 7.5 all-to-all-done.1
  125.3 33.4 %all-reduce.1 = (f32[1,768]{1,0:T(1,128)S(1)}, f32[1]{0:T(128)}) all-reduce(f32[1,768]{1,0:T(1,128)S(1)} %reduce_sum.45, f32[1]{0:T(128)} %bitcast.11), channel_id=1, replica_groups=mesh['bucket'=16,'replica'=16] {'replica'}, use_global_device_ids=true, to_apply=%region_9.10 | all-reduce | flops 769 | bytes 6152 | tf_op jit(solution)/shard_map/psum | solution.py:38
  159.5 48.9 %all-reduce.4.cloned.1.call-done = f32[1,768,768]{2,1,0:T(8,128)} async-done(((f32[1,768,768]{2,1,0:T(8,128)}), f32[1,768,768]{2,1,0:T(8,128)}) %all-reduce.4.cloned.1.call-update) | async-done | bytes 2359312 | tf_op jit(solution)/shard_map/psum | solution.py:38
  208.3 7.8 fusion.8
  216.1 6.3 fusion.214
  228.2 11.7 custom-call.67
  240.1 9.8 custom-call.68
  252.8 11.7 custom-call.69
  264.5 10.0 custom-call.70
  276.4 11.7 custom-call.71
  288.8 9.8 custom-call.72
  300.6 12.1 %custom-call.73 = f32[1,128,128]{2,1,0:T(8,128)S(1)} custom-call(f32[1,128,128]{2,1,0:T(8,128)S(1)} %cholesky.930), custom_call_target="Cholesky" | custom-call | tf_op jit(solution)/shard_map/vmap(jit(cholesky))/cholesky | solution.py:20
  313.4 9.8 custom-call.74
  325.0 11.7 custom-call.75
  337.4 9.8 custom-call.76
  348.7 11.9 custom-call.77
  369.5 17.6 %while.6 = (s32[]{:T(128)}, f32[1,768,768]{2,1,0:T(8,128)}, s32[6,2]{0,1:T(2,128)S(1)}, f32[6,1,128,128]{3,2,1,0:T(8,128)S(1)}, s32[]{:T(128)}) while((s32[]{:T(128)}, f32[1,768,768]{2,1,0:T(8,128)}, s32[6,2]{0,1:T(2,128)S(1)}, f32[6,1,128,128]{3,2,1,0:T(8,128)S(1)}, s32[]{:T(128)}) %tuple.115), condition=%wide.while_cond, body=%wide.while_body.sunk | while | flops 2 | bytes 131181 | solution.py:12
  387.1 59.0 %custom-call.78 = f32[1,6,128,128]{2,3,1,0:T(8,128)S(1)} custom-call(f32[1,6,128,128]{3,2,1,0:T(8,128)S(1)} %bitcast.892), custom_call_target="InvertDiagBlocksLowerTriangular" | custom-call | tf_op jit(solution)/shard_map/vmap(jit(_solve_triangular))/triangular_solve | solution.py:12
  459.4 4.9 fusion.90
  464.8 6.1 fusion.6
  471.0 6.5 fusion.215
  482.9 11.7 custom-call.79
  494.8 9.8 custom-call.80
  507.4 11.7 custom-call.81
  520.5 10.2 custom-call.82
  532.6 11.7 custom-call.83
  545.1 9.8 custom-call.84
  556.8 11.9 custom-call.85
  569.3 9.8 custom-call.86
  580.9 11.7 custom-call.87
  593.4 9.8 custom-call.88
  604.7 12.1 %custom-call.89 = f32[1,128,128]{2,1,0:T(8,128)S(1)} custom-call(f32[1,128,128]{2,1,0:T(8,128)S(1)} %fusion.139), custom_call_target="Cholesky" | custom-call | tf_op jit(solution)/shard_map/vmap(jit(cholesky))/cholesky | solution.py:20
  625.1 18.0 %while.7 = (s32[]{:T(128)}, f32[1,768,768]{2,1,0:T(8,128)}, s32[6,2]{0,1:T(2,128)S(1)}, f32[6,1,128,128]{3,2,1,0:T(8,128)S(1)}, s32[]{:T(128)}) while((s32[]{:T(128)}, f32[1,768,768]{2,1,0:T(8,128)}, s32[6,2]{0,1:T(2,128)S(1)}, f32[6,1,128,128]{3,2,1,0:T(8,128)S(1)}, s32[]{:T(128)}) %tuple.126), condition=%wide.while_cond.clone, body=%wide.while_body.clone.sunk | while | flops 2 | bytes 131181 | solution.py:12
  643.1 59.0 %custom-call.90 = f32[1,6,128,128]{2,3,1,0:T(8,128)S(1)} custom-call(f32[1,6,128,128]{3,2,1,0:T(8,128)S(1)} %bitcast.893), custom_call_target="InvertDiagBlocksLowerTriangular" | custom-call | tf_op jit(solution)/shard_map/vmap(jit(_solve_triangular))/triangular_solve | solution.py:12
  715.3 4.7 fusion.84
  720.5 6.1 fusion.4
  726.7 6.7 fusion.216
  738.7 11.7 custom-call.91
  750.6 9.8 custom-call.92
  763.2 11.7 custom-call.93
  776.3 9.9 custom-call.94
  788.2 11.7 custom-call.95
  800.6 9.8 custom-call.96
  812.3 12.1 %custom-call.97 = f32[1,128,128]{2,1,0:T(8,128)S(1)} custom-call(f32[1,128,128]{2,1,0:T(8,128)S(1)} %cholesky.976), custom_call_target="Cholesky" | custom-call | tf_op jit(solution)/shard_map/vmap(jit(cholesky))/cholesky | solution.py:20
  825.2 9.8 custom-call.98
  836.8 11.7 custom-call.99
  849.1 9.8 custom-call.100
  860.5 11.9 %custom-call.101 = f32[1,128,128]{2,1,0:T(8,128)S(1)} custom-call(f32[1,128,128]{2,1,0:T(8,128)S(1)} %fusion.140), custom_call_target="Cholesky" | custom-call | tf_op jit(solution)/shard_map/vmap(jit(cholesky))/cholesky | solution.py:20
  880.5 16.8 %while.8 = (s32[]{:T(128)}, f32[1,768,768]{2,1,0:T(8,128)}, s32[6,2]{0,1:T(2,128)S(1)}, f32[6,1,128,128]{3,2,1,0:T(8,128)S(1)}, s32[]{:T(128)}) while((s32[]{:T(128)}, f32[1,768,768]{2,1,0:T(8,128)}, s32[6,2]{0,1:T(2,128)S(1)}, f32[6,1,128,128]{3,2,1,0:T(8,128)S(1)}, s32[]{:T(128)}) %tuple.127), condition=%wide.while_cond.clone.1, body=%wide.while_body.clone.1.sunk | while | flops 2 | bytes 131181 | solution.py:12
  897.4 59.0 %custom-call.102 = f32[1,6,128,128]{2,3,1,0:T(8,128)S(1)} custom-call(f32[1,6,128,128]{3,2,1,0:T(8,128)S(1)} %bitcast.891), custom_call_target="InvertDiagBlocksLowerTriangular" | custom-call | tf_op jit(solution)/shard_map/vmap(jit(_solve_triangular))/triangular_solve | solution.py:12
  965.4 3.6 fusion.68
  969.5 4.7 fusion.78
  978.7 44.7 %copy.127 = bf16[1,2048,768]{2,0,1:T(2,128)(2,1)} copy(bf16[1,2048,768]{2,1,0:T(8,128)(2,1)S(1)} %fusion) | data formatting | bytes 6291456 | tf_op jit(solution)/shard_map/convert_element_type | solution.py:51
  1024.0 33.3 %reduce.53 = bf16[2048,768]{1,0:T(8,128)(2,1)} reduce(bf16[2048,1,768]{2,1,0:T(2,128)(2,1)} %bitcast.875, bf16[]{:T(256)} %broadcast.362), dimensions={1}, to_apply=%bitcast.833.reduce_sub_computation | reduce | bytes 6291458
  1057.3 6.4 reshape.753
  1063.6 79.5 %all_to_all.32 = bf16[16,2,49152]{2,1,0:T(2,128)(2,1)} all-to-all(bf16[16,2,49152]{2,1,0:T(2,128)(2,1)} %reshape.753), channel_id=1, replica_groups=mesh['bucket'=16,'replica'=16] {'bucket'}, dimensions={0} | all-to-all | bytes 6291456 | tf_op jit(solution)/shard_map/all_to_all | solution.py:52
  1143.1 11.5 reshape.754
  1154.6 5.0 copy.123
  1159.6 19.7 %gather_fusion = bf16[1024,768]{1,0:T(8,128)(2,1)} fusion(bf16[16,128,768]{2,1,0:T(8,128)(2,1)} %bitcast.852, s32[1024]{0:T(1024)S(1)} %bitcast.853), kind=kCustom, calls=%fused_computation | custom fusion | bytes 3153920 | tf_op jit(solution)/shard_map/gather | solution.py:53
  (240 shorter events, 173.4 us)
Async XLA Ops:
  6.5 201.8 %copy-start = (f32[1,768,768]{2,1,0:T(8,128)S(1)}, f32[1,768,768]{2,1,0:T(8,128)}, u32[]{:S(2)}) copy-start(f32[1,768,768]{2,1,0:T(8,128)} %param.8) | copy-start | bytes 7077892
  6.5 201.8 %all-reduce.4.cloned.1.call-start = ((), (), s32[]{:S(2)}) async-start(), calls=%async_computation.3 | async-start | bytes 4718592 | tf_op jit(solution)/shard_map/psum | solution.py:38
  104.0 1.7 copy-start.11
  110.5 11.7 all-to-all-start.1
  216.1 6.3 copy-start.4
  226.7 1.5 copy-start.15
  360.6 5.4 copy-start.8
  366.0 80.1 %copy-start.5 = (f32[768,768]{1,0:T(8,128)S(1)}, f32[768,768]{1,0:T(8,128)}, u32[]{:S(2)}) copy-start(f32[768,768]{1,0:T(8,128)} %copy-done.4) | copy-start | bytes 7077892
  458.8 6.0 copy-start.16
  471.0 6.5 copy-start.6
  481.4 1.5 copy-start.13
  616.9 4.7 copy-start.9
  621.6 80.4 %copy-start.7 = (f32[768,768]{1,0:T(8,128)S(1)}, f32[768,768]{1,0:T(8,128)}, u32[]{:S(2)}) copy-start(f32[768,768]{1,0:T(8,128)} %copy-done.6) | copy-start | bytes 7077892
  714.7 5.7 copy-start.17
  726.6 6.8 copy-start.2
  737.3 1.4 copy-start.14
  872.4 4.6 copy-start.10
  877.1 79.3 %copy-start.3 = (f32[768,768]{1,0:T(8,128)S(1)}, f32[768,768]{1,0:T(8,128)}, u32[]{:S(2)}) copy-start(f32[768,768]{1,0:T(8,128)} %copy-done.2) | copy-start | bytes 7077892
  969.5 6.3 copy-start.12
  1159.6 19.7 %copy-start.1 = (f32[1,768,768]{2,1,0:T(8,128)S(1)}, f32[1,768,768]{2,1,0:T(8,128)}, u32[]{:S(2)}) copy-start(f32[1,768,768]{2,1,0:T(8,128)} %param.8) | copy-start | bytes 7077892
Sparse Core Ops, SparseCore 0:
  109.9 98.3 all-reduce.3
where the time goes:
time: 1200 us; the launch traced here: 1190 us
  other arithmetic  611 us (51%)
  blocking collectives  194 us (16%)
  local copies, waits for them, and re-layouts  162 us (14%)
  matrix products  132 us (11%)
  waiting for transfers between devices  56.4 us (5%)
  between operations  27 us (2%)
    another operation x68, other arithmetic, orthonormal(): factor = jax.vmap(jnp.linalg.cholesky)(gram_matrix)  373 us
    another operation x7, other arithmetic, cell_solve(): return jax.scipy.linalg.solve_triangular(factor, image.T, lower=True).T  187 us
    all_to_all x1, blocking collectives, body(): lax.all_to_all(buffer, 'bucket', split_axis=0, concat_axis=1, tiled=True)  80.8 us
    all_to_all x1, blocking collectives, body(): lax.all_to_all(rotated_slots, 'bucket', split_axis=1, concat_axis=0, tile...  79.5 us
    another operation x33, matrix products, cell_solve(): return jax.scipy.linalg.solve_triangular(factor, image.T, lower=True).T  55.3 us
    another operation x58, local copies, waits for them, and re-layouts, cell_solve(): return jax.scipy.linalg.solve_triangular(factor, image.T, lower=True).T  52.1 us
    psum x1, waiting for transfers between devices, body(): lax.psum((count_part, sum_part, square_part), 'replica')  48.9 us
    convert_element_type x1, local copies, waits for them, and re-layouts, body(): rotated_slots = (product - shift[:, None, :]).astype(jnp.bfloat16)  44.7 us
  transfers between devices with their start and end apart: 2, of which 2 were waited for; matrix products, arithmetic and copies ran while one was open for 0% of the time, Pallas kernels for 0%

commit v1 on v0

v1 whole, which is shorter than its diff:
```python
import functools

import jax
import jax.numpy as jnp
from jax import lax
from jax.experimental import pallas as pl
from jax.experimental.pallas import tpu as pltpu
from jax.sharding import PartitionSpec as P

CELLS = 16
SWEEPS = 3
CAP = 128
D = 768
RB = 128
NB = D // RB
ROWS = 1024
SLOTS = CELLS * CAP
F32 = jnp.float32
BF16 = jnp.bfloat16
NT = (((1,), (1,)), ((), ()))
TN = (((0,), (0,)), ((), ()))
VMEM = pl.BlockSpec(memory_space=pltpu.VMEM)


def params(mib, **kw):
    return pltpu.CompilerParams(vmem_limit_bytes=mib * 2**20, **kw)


def dot(a, b):
    return jnp.dot(a, b, preferred_element_type=F32)


def dot_nt(a, b):
    return lax.dot_general(a, b, NT, preferred_element_type=F32)


def halves(x):
    high = x.astype(BF16)
    return high, (x - high.astype(F32)).astype(BF16)


def dispatch_kernel(ids_ref, rows_ref, buffer_ref, counts_ref, place_ref):
    ids = ids_ref[...]
    cells = lax.broadcasted_iota(jnp.int32, (CELLS, ROWS), 0)
    onehot = (ids == cells).astype(F32)
    before = (
        lax.broadcasted_iota(jnp.int32, (ROWS, ROWS), 0)
        < lax.broadcasted_iota(jnp.int32, (ROWS, ROWS), 1)
    ).astype(F32).astype(BF16)
    ranks = dot(onehot.astype(BF16), before)
    slot = jnp.sum(ranks * onehot, axis=0, keepdims=True).astype(jnp.int32)
    place = ids * CAP + slot
    counts_ref[...] = jnp.broadcast_to(jnp.sum(onehot, axis=1, keepdims=True), (CELLS, 128))
    place_ref[...] = jnp.broadcast_to(place, (128, ROWS)).T

    def fill(cell, carry):
        wanted = lax.broadcasted_iota(jnp.int32, (CAP, ROWS), 0) + cell * CAP
        pick = (place == wanted).astype(F32).astype(BF16)
        first = pl.multiple_of(cell * CAP, CAP)
        buffer_ref[pl.ds(first, CAP), :] = dot(pick, rows_ref[...]).astype(BF16)
        return carry

    lax.fori_loop(0, CELLS, fill, 0)


def moments_kernel(received_ref, counts_ref, out_ref):
    for block in range(D // 256):
        columns = pl.ds(block * 256, 256)
        out_ref[columns, :] = lax.dot_general(
            received_ref[:, columns], received_ref[...], TN, preferred_element_type=F32
        )
    ones = jnp.ones((8, SLOTS), BF16)
    total = dot(ones, received_ref[...])
    count = jnp.sum(counts_ref[...])
    is_total = lax.broadcasted_iota(jnp.int32, (8, D), 0) == 0
    out_ref[D : D + 8, :] = jnp.where(is_total, total, count)


def factor(a_ref, m_ref):
    n = RB // 8
    shape = (8, RB)
    sub = lax.broadcasted_iota(jnp.int32, shape, 0)
    lane = lax.broadcasted_iota(jnp.int32, shape, 1)
    a = [a_ref[8 * r : 8 * r + 8, :] for r in range(n)]
    m = [(lane == sub + 8 * r).astype(F32) for r in range(n)]
    for b in range(n):
        col = [
            [jnp.broadcast_to(a[r][:, 8 * b + j : 8 * b + j + 1], shape) for j in range(8)]
            if r >= b
            else None
            for r in range(n)
        ]
        s = [
            [jnp.broadcast_to(col[b][j][i : i + 1, :], shape) if i >= j else None for j in range(8)]
            for i in range(8)
        ]
        t = [[None] * 8 for _ in range(8)]
        inverse = [None] * 8
        for j in range(8):
            inverse[j] = 1.0 / s[j][j]
            for i in range(j + 1, 8):
                t[i][j] = s[i][j] * inverse[j]
            for k in range(j + 1, 8):
                for i in range(k, 8):
                    s[i][k] = s[i][k] - t[k][j] * s[i][j]
        low = [[None] * 8 for _ in range(n)]
        for r in range(b, n):
            for j in range(8):
                for i in range(j + 1, 8):
                    col[r][i] = col[r][i] - col[r][j] * t[i][j]
                low[r][j] = col[r][j] * inverse[j]
        panel, inv_panel = a[b], m[b]
        rows, inv_rows = [], []
        for j in range(8):
            rows.append(jnp.broadcast_to(panel[j : j + 1, :], shape))
            inv_rows.append(jnp.broadcast_to(inv_panel[j : j + 1, :], shape))
            if j < 7:
                below = jnp.where(sub > j, low[b][j], 0.0)
                panel = panel - below * rows[j]
                inv_panel = inv_panel - below * inv_rows[j]
        pivots = s[0][0]
        for j in range(1, 8):
            pivots = jnp.where(sub == j, s[j][j], pivots)
        m[b] = inv_panel * lax.rsqrt(pivots)
        for r in range(b + 1, n):
            for j in range(8):
                a[r] = a[r] - low[r][j] * rows[j]
                m[r] = m[r] - low[r][j] * inv_rows[j]
    for r in range(n):
        m_ref[8 * r : 8 * r + 8, :] = m[r]


def sweeps_kernel(
    reduced_ref, start_ref, w_high, shift_ref, c_high, c_low, y, y_high, y_low, w_low, gram, inverse
):
    tail = reduced_ref[D : D + 8, :]
    divisor = jnp.maximum(tail[1:2, :], 1.0)
    mean = tail[0:1, :] / divisor
    first = lax.broadcasted_iota(jnp.int32, (8, D), 0) == 0
    mean_rows = jnp.where(first, jnp.broadcast_to(mean, (8, D)), 0.0)
    for block in range(NB):
        span = slice(block * RB, block * RB + RB)
        outer = lax.dot_general(
            mean_rows[:, span], mean_rows, TN, preferred_element_type=F32,
            precision=lax.Precision.HIGHEST,
        )
        high, low = halves(reduced_ref[span, :] / divisor - outer)
        c_high[span, :] = high
        c_low[span, :] = low
        high, low = halves(start_ref[:, span].T)
        w_high[span, :] = high
        w_low[span, :] = low

    def sweep(step, carry):
        for block in range(D // 256):
            span = slice(block * 256, block * 256 + 256)
            image = (
                dot(w_high[span, :], c_high[...])
                + dot(w_high[span, :], c_low[...])
                + dot(w_low[span, :], c_high[...])
            )
            y[span, :] = image
            high, low = halves(image)
            y_high[span, :] = high
            y_low[span, :] = low

        def block_step(block, inner):
            span = pl.ds(pl.multiple_of(block * RB, RB), RB)
            high, low = y_high[span, :], y_low[span, :]
            gram[...] = dot_nt(high, high) + dot_nt(high, low) + dot_nt(low, high)
            factor(gram, inverse)
            i_high, i_low = halves(inverse[...])
            w_h, w_l = halves(dot(i_high, high) + dot(i_high, low) + dot(i_low, high))
            w_high[span, :] = w_h
            w_low[span, :] = w_l
            for done in range(NB - 1):

                @pl.when(block == done)
                def _():
                    rest = slice(RB * (done + 1), D)
                    own = slice(RB * done, RB * done + RB)
                    u_h, u_l = w_high[own, :], w_low[own, :]
                    r_h, r_l = y_high[rest, :], y_low[rest, :]
                    l_h, l_l = halves(dot_nt(r_h, u_h) + dot_nt(r_h, u_l) + dot_nt(r_l, u_h))
                    left = y[rest, :] - (dot(l_h, u_h) + dot(l_h, u_l) + dot(l_l, u_h))
                    y[rest, :] = left
                    high, low = halves(left)
                    y_high[rest, :] = high
                    y_low[rest, :] = low

            return inner

        return lax.fori_loop(0, NB, block_step, carry)

    lax.fori_loop(0, SWEEPS, sweep, 0)
    shift_ref[...] = lax.dot_general(
        jnp.broadcast_to(mean, (8, D)), w_high[...].astype(F32), NT,
        preferred_element_type=F32, precision=lax.Precision.HIGHEST,
    )


def rotate_kernel(received_ref, w_ref, shift_ref, out_ref):
    def step(index, carry):
        span = pl.ds(pl.multiple_of(index * 256, 256), 256)
        product = dot_nt(received_ref[span, :], w_ref[...])
        out_ref[span, :] = (product - shift_ref[0:1, :]).astype(BF16)
        return carry

    lax.fori_loop(0, SLOTS // 256, step, 0)


def collect_kernel(returned_ref, place_ref, out_ref):
    def step(index, carry):
        span = pl.ds(pl.multiple_of(index * 256, 256), 256)
        place = place_ref[span, :]
        lane = lax.broadcasted_iota(jnp.int32, (256, CAP), 1)
        pick = jnp.concatenate(
            [(place == lane + cell * CAP).astype(F32).astype(BF16) for cell in range(CELLS)], axis=1
        )
        out_ref[span, :] = dot(pick, returned_ref[...]).astype(BF16)
        return carry

    lax.fori_loop(0, ROWS // 256, step, 0)


def sweeps(reduced, start):
    return pl.pallas_call(
        sweeps_kernel,
        out_shape=[jax.ShapeDtypeStruct((D, D), BF16), jax.ShapeDtypeStruct((8, D), F32)],
        in_specs=[VMEM, VMEM],
        out_specs=[VMEM, VMEM],
        scratch_shapes=[
            pltpu.VMEM((D, D), BF16),
            pltpu.VMEM((D, D), BF16),
            pltpu.VMEM((D, D), F32),
            pltpu.VMEM((D, D), BF16),
            pltpu.VMEM((D, D), BF16),
            pltpu.VMEM((D, D), BF16),
            pltpu.VMEM((RB, RB), F32),
            pltpu.VMEM((RB, RB), F32),
        ],
        compiler_params=params(48),
        name="sweeps",
    )(reduced, start)


def body(rows, cell_ids, start_basis):
    buffer, counts, place = pl.pallas_call(
        dispatch_kernel,
        out_shape=[
            jax.ShapeDtypeStruct((SLOTS, D), BF16),
            jax.ShapeDtypeStruct((CELLS, 128), F32),
            jax.ShapeDtypeStruct((ROWS, 128), jnp.int32),
        ],
        in_specs=[VMEM, VMEM],
        out_specs=[VMEM] * 3,
        compiler_params=params(40),
        name="dispatch",
    )(cell_ids.reshape(1, ROWS), rows)
    received = lax.all_to_all(buffer, "bucket", split_axis=0, concat_axis=0, tiled=True)
    recv_counts = lax.all_to_all(counts[:, :1], "bucket", split_axis=0, concat_axis=0, tiled=True)
    partial = pl.pallas_call(
        moments_kernel,
        out_shape=jax.ShapeDtypeStruct((D + 8, D), F32),
        in_specs=[VMEM, VMEM],
        out_specs=VMEM,
        compiler_params=params(40),
        name="moments",
    )(received, recv_counts)
    reduced = lax.psum(partial, "replica")
    rotation, shift = sweeps(reduced, start_basis[0])
    rotated = pl.pallas_call(
        rotate_kernel,
        out_shape=jax.ShapeDtypeStruct((SLOTS, D), BF16),
        in_specs=[VMEM] * 3,
        out_specs=VMEM,
        compiler_params=params(40),
        name="rotate",
    )(received, rotation, shift)
    returned = lax.all_to_all(rotated, "bucket", split_axis=0, concat_axis=0, tiled=True)
    return pl.pallas_call(
        collect_kernel,
        out_shape=jax.ShapeDtypeStruct((ROWS, D), BF16),
        in_specs=[VMEM] * 2,
        out_specs=VMEM,
        compiler_params=params(40),
        name="collect",
    )(returned, place)


def solution(mesh):
    both = P(("bucket", "replica"), None)
    return jax.shard_map(
        body,
        mesh=mesh,
        in_specs=(both, both, P("bucket", None, None)),
        out_specs=both,
        check_vma=False,
    )
```

time: 1200 us -> 456 us (0.38)
  other arithmetic: 611 us -> 0 us
  Pallas kernels: 0 us -> 163 us
  local copies, waits for them, and re-layouts: 162 us -> 6.87 us
  matrix products: 132 us -> 0 us
  waiting for transfers between devices: 56.4 us -> 98.2 us
  blocking collectives: 194 us -> 170 us
  between operations: 27 us -> 13.4 us
    another operation x78 -> x0, other arithmetic: 565 us -> none  [the longest x68 373 us: orthonormal(): factor = jax.vmap(jnp.linalg.cholesky)(gram_matrix)]
    pallas_call x0 -> x5, Pallas kernels: none -> 163 us  [the longest x1 144 us: sweeps(): pl.pallas_call(sweeps_kernel, out_shape=[jax.ShapeDtypeStruct((D, D), BF1...]
    another operation x63 -> x0, matrix products: 84.7 us -> none  [the longest x33 55.3 us: cell_solve(): return jax.scipy.linalg.solve_triangular(factor, image.T, lower=True).T]
    another operation x80 -> x0, local copies, waits for them, and re-layouts: 53 us -> none  [the longest x58 52.1 us: cell_solve(): return jax.scipy.linalg.solve_triangular(factor, image.T, lower=True).T]
    psum x1, waiting for transfers between devices: 48.9 us -> 98.2 us  [body(): reduced = lax.psum(partial, 'replica')]
    dot_general x9 -> x0, matrix products: 47.7 us -> none  [the longest x3 20.1 us: body(): jnp.einsum('cij,cjk->cik', covariance, current, precision=lax.Precision.H...]
    convert_element_type x2 -> x0, local copies, waits for them, and re-layouts: 45.4 us -> none  [the longest x1 44.7 us: body(): rotated_slots = (product - shift[:, None, :]).astype(jnp.bfloat16)]
    unnamed x4 -> x0, other arithmetic: 34.8 us -> none
  transfers between devices with their start and end apart: 2 -> 1, of which waited for: 2 -> 1; matrix products, arithmetic and copies ran while one was open for 0% -> 0% of each run, Pallas kernels for 0% -> 0%
where the time goes in v1:
time: 456 us; the launch traced here: 451 us
  blocking collectives  170 us (37%)
  Pallas kernels  163 us (36%)
  waiting for transfers between devices  98.2 us (22%)
  between operations  13.4 us (3%)
  local copies, waits for them, and re-layouts  6.87 us (2%)
    pallas_call x1, Pallas kernels, sweeps(): pl.pallas_call(sweeps_kernel, out_shape=[jax.ShapeDtypeStruct((D, D), BF1...  144 us
    psum x1, waiting for transfers between devices, body(): reduced = lax.psum(partial, 'replica')  98.2 us
    all_to_all x1, blocking collectives, body(): lax.all_to_all(rotated, 'bucket', split_axis=0, concat_axis=0, tiled=True)  79.3 us
    all_to_all x1, blocking collectives, body(): lax.all_to_all(buffer, 'bucket', split_axis=0, concat_axis=0, tiled=True)  74.8 us
    all_to_all x1, blocking collectives, body(): lax.all_to_all(counts[:, :1], 'bucket', split_axis=0, concat_axis=0, tile...  15.9 us
  transfers between devices with their start and end apart: 1, of which 1 were waited for; matrix products, arithmetic and copies ran while one was open for 0% of the time, Pallas kernels for 0%

profile of v1, /device:TPU:26, one launch (start us, length us, event | category | flops | bytes accessed | tf_op | source)
XLA Modules:
  0.0 451.0 jit_solution(12177900624537165737)
XLA Ops:
  6.5 0.0 all-reduce.2.cloned.1.call-start
  6.5 0.0 copy-start.3
  6.5 1.4 copy-done.3
  7.9 0.0 copy-start.6
  7.9 0.7 copy-done.6
  8.6 6.6 %dispatch.1 = (bf16[2048,768]{1,0:T(8,128)(2,1)S(1)}, f32[16,128]{1,0:T(8,128)S(1)}, s32[1024,128]{1,0:T(8,128)S(1)}) custom-call(s32[1,1024]{1,0:T(1,128)S(1)} %bitcast.17, bf16[1024,768]{1,0:T(8,128)(2,1)S(1)} %copy-done.3), custom_call_target="tpu_custom_call" | custom-call | tf_op jit(solution)/shard_map/dispatch/pallas_call | solution.py:248
  15.2 0.0 copy-start.4
  15.2 15.9 %all_to_all.33 = f32[16,1,1]{2,1,0:T(1,128)S(1)} all-to-all(f32[16,1,1]{2,1,0:T(1,128)S(1)} %bitcast.16), channel_id=1, replica_groups=mesh['bucket'=16,'replica'=16] {'bucket'}, dimensions={0} | all-to-all | bytes 128 | tf_op jit(solution)/shard_map/all_to_all | solution.py:261
  31.2 74.8 %all_to_all.34 = bf16[16,128,768]{2,1,0:T(8,128)(2,1)S(1)} all-to-all(bf16[16,128,768]{2,1,0:T(8,128)(2,1)S(1)} %bitcast.13), channel_id=1, replica_groups=mesh['bucket'=16,'replica'=16] {'bucket'}, dimensions={0} | all-to-all | bytes 6291456 | tf_op jit(solution)/shard_map/all_to_all | solution.py:260
  105.9 0.0 copy-done.4
  106.0 3.0 moments.1
  109.0 0.0 copy-start
  109.0 1.4 copy-done
  110.4 0.0 all-reduce.2.cloned.1.call-update
  110.4 98.2 %all-reduce.2.cloned.1.call-done.reduced_ref = f32[776,768]{1,0:T(8,128)} async-done(((f32[776,768]{1,0:T(8,128)}), f32[776,768]{1,0:T(8,128)}) %all-reduce.2.cloned.1.call-update) | async-done | bytes 2383888 | tf_op jit(solution)/shard_map/psum | solution.py:270
  208.6 0.0 copy-start.1
  208.6 1.7 copy-done.1
  210.3 0.0 copy-start.2
  210.3 1.7 copy-done.2
  212.0 143.7 %sweeps.1 = (bf16[768,768]{1,0:T(8,128)(2,1)S(1)}, f32[8,768]{1,0:T(8,128)S(1)}) custom-call(f32[776,768]{1,0:T(8,128)S(1)} %copy-done.1, f32[768,768]{1,0:T(8,128)S(1)} %bitcast.14), custom_call_target="tpu_custom_call" | custom-call | tf_op jit(solution)/shard_map/sweeps/pallas_call | solution.py:227
  355.7 4.1 rotate.1
  359.8 0.0 copy-start.5
  359.8 79.3 %all_to_all.35 = bf16[16,128,768]{2,1,0:T(8,128)(2,1)S(1)} all-to-all(bf16[16,128,768]{2,1,0:T(8,128)(2,1)S(1)} %bitcast.11), channel_id=1, replica_groups=mesh['bucket'=16,'replica'=16] {'bucket'}, dimensions={0} | all-to-all | bytes 6291456 | tf_op jit(solution)/shard_map/all_to_all | solution.py:280
  439.1 0.0 copy-done.5
  439.1 5.1 %collect.1 = bf16[1024,768]{1,0:T(8,128)(2,1)} custom-call(bf16[2048,768]{1,0:T(8,128)(2,1)S(1)} %bitcast.12, s32[1024,128]{1,0:T(8,128)S(1)} %copy-done.5), custom_call_target="tpu_custom_call" | custom-call | tf_op jit(solution)/shard_map/collect/pallas_call | solution.py:281
Async XLA Ops:
  6.5 202.1 %all-reduce.2.cloned.1.call-start = ((), (), s32[]{:S(2)}) async-start(), calls=%async_computation.3 | async-start | bytes 4767744 | tf_op jit(solution)/shard_map/psum | solution.py:270
  6.5 1.4 copy-start.3
  7.9 0.7 copy-start.6
  15.2 90.7 %copy-start.4 = (s32[1024,128]{1,0:T(8,128)}, s32[1024,128]{1,0:T(8,128)S(1)}, u32[]{:S(2)}) copy-start(s32[1024,128]{1,0:T(8,128)S(1)} %get-tuple-element.14.place_ref) | copy-start | bytes 1572868
  109.0 1.4 copy-start
  208.6 1.7 copy-start.1
  210.3 1.7 copy-start.2
  359.8 79.3 %copy-start.5 = (s32[1024,128]{1,0:T(8,128)S(1)}, s32[1024,128]{1,0:T(8,128)}, u32[]{:S(2)}) copy-start(s32[1024,128]{1,0:T(8,128)} %copy-done.4) | copy-start | bytes 1572868
Sparse Core Ops, SparseCore 0:
  110.6 98.0 all-reduce.1

commit v2 on v1

--- a/solution.py
+++ b/solution.py
@@ -20,6 +20,18 @@
 NT = (((1,), (1,)), ((), ()))
 TN = (((0,), (0,)), ((), ()))
 VMEM = pl.BlockSpec(memory_space=pltpu.VMEM)
+ANY = pl.BlockSpec(memory_space=pl.ANY)
+MESH = pl.DeviceIdType.MESH
+DMA = pltpu.SemaphoreType.DMA
+PLANE = 16
+RING = 8
+PAIRS = [(i, j) for i in range(NB) for j in range(i, NB)]
+CHUNK = 176
+HALF = RING * CHUNK
+PACKED = 2 * HALF
+TAIL = len(PAIRS) * RB
+PIECES = 12
+PIECE = D // PIECES
 
 
 def params(mib, **kw):
@@ -50,7 +62,9 @@
     ranks = dot(onehot.astype(BF16), before)
     slot = jnp.sum(ranks * onehot, axis=0, keepdims=True).astype(jnp.int32)
     place = ids * CAP + slot
-    counts_ref[...] = jnp.broadcast_to(jnp.sum(onehot, axis=1, keepdims=True), (CELLS, 128))
+    eighth = lax.broadcasted_iota(jnp.int32, (8 * CELLS, ROWS), 0) // 8
+    each = jnp.sum((ids == eighth).astype(F32), axis=1, keepdims=True)
+    counts_ref[...] = jnp.broadcast_to(each, (8 * CELLS, 128))
     place_ref[...] = jnp.broadcast_to(place, (128, ROWS)).T
 
     def fill(cell, carry):
@@ -63,17 +77,229 @@
     lax.fori_loop(0, CELLS, fill, 0)
 
 
+def scatter_kernel(
+    buffer_ref, counts_ref, basis_ref, received_ref, got_counts_ref, got_basis_ref,
+    send, recv, send_count, recv_count, send_up, send_down, send_across, recv_chain, recv_across, own
+):
+    bucket, me = lax.axis_index("bucket"), lax.axis_index("replica")
+    z, core = bucket // 2, bucket % 2
+    origin, chain_core = me // 2, me % 2
+    away = lax.rem(z + RING - origin, RING)
+    up = lax.rem(z + 1, RING) * 2 + core
+    down = lax.rem(z + RING - 1, RING) * 2 + core
+    across = z * 2 + (1 - core)
+    peers = plane_peers(me)
+
+    barrier = pltpu.get_barrier_semaphore()
+    for peer in peers:
+        pl.semaphore_signal(barrier, inc=1, device_id=(bucket, peer), device_id_type=MESH)
+    for other in (up, down, across):
+        pl.semaphore_signal(barrier, inc=1, device_id=(other, me), device_id_type=MESH)
+    pl.semaphore_wait(barrier, len(peers) + 3)
+
+    copies = []
+    for index, peer in enumerate(peers):
+        copies.append(pltpu.make_async_remote_copy(
+            counts_ref.at[pl.ds(pl.multiple_of(peer * 8, 8), 8)],
+            got_counts_ref.at[pl.ds(pl.multiple_of(me * 8, 8), 8)],
+            send_count.at[index], recv_count.at[index], device_id=(bucket, peer), device_id_type=MESH,
+        ))
+        copies.append(exchange(buffer_ref, received_ref, send, recv, index, bucket, me, peer))
+    for copy in copies:
+        copy.start()
+    mine = pl.ds(pl.multiple_of(me * CAP, CAP), CAP)
+    mine_counts = pl.ds(pl.multiple_of(me * 8, 8), 8)
+    local = [
+        pltpu.make_async_copy(buffer_ref.at[mine], received_ref.at[mine], own.at[0]),
+        pltpu.make_async_copy(counts_ref.at[mine_counts], got_counts_ref.at[mine_counts], own.at[1]),
+    ]
+    for copy in local:
+        copy.start()
+
+    def passing(source, index, sends, receives, target):
+        span = pl.ds(index * PIECE, PIECE)
+        return pltpu.make_async_remote_copy(
+            source.at[span], got_basis_ref.at[span], sends.at[index], receives.at[index],
+            device_id=(target, me), device_id_type=MESH,
+        )
+
+    on_chain = core == chain_core
+    first = on_chain & (away == 0)
+    later = on_chain & (away > 0)
+
+    @pl.when(first)
+    def _():
+        whole = pltpu.make_async_copy(basis_ref, got_basis_ref, own.at[2])
+        whole.start()
+        for index in range(PIECES):
+            passing(basis_ref, index, send_up, recv_chain, up).start()
+            passing(basis_ref, index, send_down, recv_chain, down).start()
+            passing(basis_ref, index, send_across, recv_across, across).start()
+        for index in range(PIECES):
+            passing(basis_ref, index, send_up, recv_chain, up).wait_send()
+            passing(basis_ref, index, send_down, recv_chain, down).wait_send()
+            passing(basis_ref, index, send_across, recv_across, across).wait_send()
+        whole.wait()
+
+    @pl.when(later)
+    def _():
+        upward = away < 4
+        downward = away > 5
+        for index in range(PIECES):
+            passing(got_basis_ref, index, send_up, recv_chain, up).wait_recv()
+
+            @pl.when(upward)
+            def _():
+                passing(got_basis_ref, index, send_up, recv_chain, up).start()
+
+            @pl.when(downward)
+            def _():
+                passing(got_basis_ref, index, send_down, recv_chain, down).start()
+
+            passing(got_basis_ref, index, send_across, recv_across, across).start()
+        for index in range(PIECES):
+            @pl.when(upward)
+            def _():
+                passing(got_basis_ref, index, send_up, recv_chain, up).wait_send()
+
+            @pl.when(downward)
+            def _():
+                passing(got_basis_ref, index, send_down, recv_chain, down).wait_send()
+
+            passing(got_basis_ref, index, send_across, recv_across, across).wait_send()
+
+    @pl.when(core != chain_core)
+    def _():
+        for index in range(PIECES):
+            passing(got_basis_ref, index, send_across, recv_across, across).wait_recv()
+
+    for copy in copies + local:
+        copy.wait()
+
+
+def plane_peers(me):
+    y, x = me // 4, me % 4
+    return [
+        lax.rem(y + dy, 4) * 4 + lax.rem(x + dx, 4)
+        for dy, dx in sorted(
+            ((dy, dx) for dy in range(4) for dx in range(4) if dy or dx),
+            key=lambda o: -min(o[0], 4 - o[0]) - min(o[1], 4 - o[1]),
+        )
+    ]
+
+
+def exchange(source, target, send, recv, index, bucket, me, peer):
+    return pltpu.make_async_remote_copy(
+        source.at[pl.ds(pl.multiple_of(peer * CAP, CAP), CAP)],
+        target.at[pl.ds(pl.multiple_of(me * CAP, CAP), CAP)],
+        send.at[index], recv.at[index], device_id=(bucket, peer), device_id_type=MESH,
+    )
+
+
+def giveback_kernel(rotated_ref, returned_ref, send, recv, own):
+    bucket, me = lax.axis_index("bucket"), lax.axis_index("replica")
+    peers = plane_peers(me)
+    barrier = pltpu.get_barrier_semaphore()
+    for peer in peers:
+        pl.semaphore_signal(barrier, inc=1, device_id=(bucket, peer), device_id_type=MESH)
+    pl.semaphore_wait(barrier, len(peers))
+    copies = [
+        exchange(rotated_ref, returned_ref, send, recv, index, bucket, me, peer)
+        for index, peer in enumerate(peers)
+    ]
+    mine = pl.ds(pl.multiple_of(me * CAP, CAP), CAP)
+    copies.append(pltpu.make_async_copy(rotated_ref.at[mine], returned_ref.at[mine], own.at[0]))
+    for copy in copies:
+        copy.start()
+    for copy in copies:
+        copy.wait()
+
+
 def moments_kernel(received_ref, counts_ref, out_ref):
-    for block in range(D // 256):
-        columns = pl.ds(block * 256, 256)
-        out_ref[columns, :] = lax.dot_general(
-            received_ref[:, columns], received_ref[...], TN, preferred_element_type=F32
-        )
-    ones = jnp.ones((8, SLOTS), BF16)
-    total = dot(ones, received_ref[...])
-    count = jnp.sum(counts_ref[...])
-    is_total = lax.broadcasted_iota(jnp.int32, (8, D), 0) == 0
-    out_ref[D : D + 8, :] = jnp.where(is_total, total, count)
+    place = 0
+    for block in range(NB):
+        rest = slice(block * RB, D)
+        square = lax.dot_general(
+            received_ref[:, block * RB : block * RB + RB], received_ref[:, rest], TN,
+            preferred_element_type=F32,
+        )
+        for other in range(NB - block):
+            out_ref[place : place + RB, :] = square[:, other * RB : other * RB + RB]
+            place += RB
+    total = dot(jnp.ones((8, SLOTS), BF16), received_ref[...])
+    out_ref[TAIL:PACKED, :] = jnp.zeros((PACKED - TAIL, RB), F32)
+    for block in range(NB):
+        out_ref[TAIL + block : TAIL + block + 1, :] = total[0:1, block * RB : block * RB + RB]
+    count = jnp.sum(counts_ref[...].reshape(CELLS, 8, 128)[:, 0, :], axis=0, keepdims=True)
+    out_ref[TAIL + NB : TAIL + NB + 1, :] = count
+
+
+def reduce_kernel(
+    part_ref, out_ref, full, arrived, mine, slots, send_half, recv_half, send_part, recv_part,
+    send_all, recv_all, send_across, recv_across
+):
+    bucket, me = lax.axis_index("bucket"), lax.axis_index("replica")
+    z, core = bucket // 2, bucket % 2
+    across = (z * 2 + (1 - core), me)
+    ring = [(lax.rem(z + step, RING) * 2 + core, me) for step in range(RING)]
+    barrier = pltpu.get_barrier_semaphore()
+    for other in [across] + ring[1:]:
+        pl.semaphore_signal(barrier, inc=1, device_id=other, device_id_type=MESH)
+    pl.semaphore_wait(barrier, RING)
+
+    half = pltpu.make_async_remote_copy(
+        part_ref.at[pl.ds(pl.multiple_of((1 - core) * HALF, 8), HALF)], arrived,
+        send_half, recv_half, device_id=across, device_id_type=MESH,
+    )
+    half.start()
+    half.wait()
+    mine[...] = part_ref[pl.ds(pl.multiple_of(core * HALF, 8), HALF), :] + arrived[...]
+
+    order = [4, 3, 5, 2, 6, 1, 7]
+    parts = []
+    for step in order:
+        chunk = lax.rem(z + step, RING)
+        parts.append(pltpu.make_async_remote_copy(
+            mine.at[pl.ds(pl.multiple_of(chunk * CHUNK, 8), CHUNK)], slots.at[step],
+            send_part.at[step], recv_part.at[step], device_id=ring[step], device_id_type=MESH,
+        ))
+    for copy in parts:
+        copy.start()
+    total = mine[pl.ds(pl.multiple_of(z * CHUNK, 8), CHUNK), :]
+    for step, copy in zip(order, parts):
+        copy.wait_recv()
+        total = total + slots[step]
+
+    def chunk_of(where):
+        return pl.ds(pl.multiple_of((core * RING + where) * CHUNK, 8), CHUNK)
+
+    full[chunk_of(z), :] = total
+    spread = [
+        pltpu.make_async_remote_copy(
+            full.at[chunk_of(z)], full.at[chunk_of(z)], send_all.at[step], recv_all.at[step],
+            device_id=ring[step], device_id_type=MESH,
+        )
+        for step in order
+    ]
+    for copy in spread:
+        copy.start()
+
+    def forward(step):
+        where = chunk_of(lax.rem(z + RING - step, RING))
+        return pltpu.make_async_remote_copy(
+            full.at[where], full.at[where], send_across.at[step], recv_across.at[step],
+            device_id=across, device_id_type=MESH,
+        )
+
+    forward(0).start()
+    for step, copy in sorted(zip(order, spread), key=lambda item: min(item[0], RING - item[0])):
+        copy.wait_recv()
+        forward(step).start()
+    for step in range(RING):
+        forward(step).wait()
+    for copy in parts + spread:
+        copy.wait_send()
+    out_ref[...] = full[...]
 
 
 def factor(a_ref, m_ref):
@@ -133,9 +359,11 @@
 def sweeps_kernel(
     reduced_ref, start_ref, w_high, shift_ref, c_high, c_low, y, y_high, y_low, w_low, gram, inverse
 ):
-    tail = reduced_ref[D : D + 8, :]
-    divisor = jnp.maximum(tail[1:2, :], 1.0)
-    mean = tail[0:1, :] / divisor
+    count = reduced_ref[TAIL + NB : TAIL + NB + 1, :]
+    divisor = jnp.maximum(count, 1.0)
+    mean = jnp.concatenate(
+        [reduced_ref[TAIL + block : TAIL + block + 1, :] / divisor for block in range(NB)], axis=1
+    )
     first = lax.broadcasted_iota(jnp.int32, (8, D), 0) == 0
     mean_rows = jnp.where(first, jnp.broadcast_to(mean, (8, D)), 0.0)
     for block in range(NB):
@@ -144,9 +372,15 @@
             mean_rows[:, span], mean_rows, TN, preferred_element_type=F32,
             precision=lax.Precision.HIGHEST,
         )
-        high, low = halves(reduced_ref[span, :] / divisor - outer)
-        c_high[span, :] = high
-        c_low[span, :] = low
+        for other in range(NB):
+            columns = slice(other * RB, other * RB + RB)
+            place = PAIRS.index((min(block, other), max(block, other))) * RB
+            piece = reduced_ref[place : place + RB, :]
+            if other < block:
+                piece = piece.T
+            high, low = halves(piece / divisor - outer[:, columns])
+            c_high[span, columns] = high
+            c_low[span, columns] = low
         high, low = halves(start_ref[:, span].T)
         w_high[span, :] = high
         w_low[span, :] = low
@@ -244,12 +478,16 @@
     )(reduced, start)
 
 
+def remote(identity):
+    return params(40, collective_id=identity, has_side_effects=True)
+
+
 def body(rows, cell_ids, start_basis):
     buffer, counts, place = pl.pallas_call(
         dispatch_kernel,
         out_shape=[
             jax.ShapeDtypeStruct((SLOTS, D), BF16),
-            jax.ShapeDtypeStruct((CELLS, 128), F32),
+            jax.ShapeDtypeStruct((8 * CELLS, 128), F32),
             jax.ShapeDtypeStruct((ROWS, 128), jnp.int32),
         ],
         in_specs=[VMEM, VMEM],
@@ -257,18 +495,43 @@
         compiler_params=params(40),
         name="dispatch",
     )(cell_ids.reshape(1, ROWS), rows)
-    received = lax.all_to_all(buffer, "bucket", split_axis=0, concat_axis=0, tiled=True)
-    recv_counts = lax.all_to_all(counts[:, :1], "bucket", split_axis=0, concat_axis=0, tiled=True)
+    received, got_counts, basis = pl.pallas_call(
+        scatter_kernel,
+        out_shape=[
+            jax.ShapeDtypeStruct((SLOTS, D), BF16),
+            jax.ShapeDtypeStruct((8 * CELLS, 128), F32),
+            jax.ShapeDtypeStruct((D, D), F32),
+        ],
+        in_specs=[ANY] * 3,
+        out_specs=[ANY] * 3,
+        scratch_shapes=[DMA((PLANE - 1,))] * 4 + [DMA((PIECES,))] * 5 + [DMA((3,))],
+        compiler_params=remote(1),
+        name="scatter",
+    )(buffer, counts, start_basis[0])
     partial = pl.pallas_call(
         moments_kernel,
-        out_shape=jax.ShapeDtypeStruct((D + 8, D), F32),
+        out_shape=jax.ShapeDtypeStruct((PACKED, RB), F32),
         in_specs=[VMEM, VMEM],
         out_specs=VMEM,
         compiler_params=params(40),
         name="moments",
-    )(received, recv_counts)
-    reduced = lax.psum(partial, "replica")
-    rotation, shift = sweeps(reduced, start_basis[0])
+    )(received, got_counts)
+    reduced = pl.pallas_call(
+        reduce_kernel,
+        out_shape=jax.ShapeDtypeStruct((PACKED, RB), F32),
+        in_specs=[VMEM],
+        out_specs=VMEM,
+        scratch_shapes=[
+            pltpu.VMEM((PACKED, RB), F32),
+            pltpu.VMEM((HALF, RB), F32),
+            pltpu.VMEM((HALF, RB), F32),
+            pltpu.VMEM((RING, CHUNK, RB), F32),
+            DMA, DMA,
+        ] + [DMA((RING,))] * 6,
+        compiler_params=remote(2),
+        name="reduce",
+    )(partial)
+    rotation, shift = sweeps(reduced, basis)
     rotated = pl.pallas_call(
         rotate_kernel,
         out_shape=jax.ShapeDtypeStruct((SLOTS, D), BF16),
@@ -277,7 +540,15 @@
         compiler_params=params(40),
         name="rotate",
     )(received, rotation, shift)
-    returned = lax.all_to_all(rotated, "bucket", split_axis=0, concat_axis=0, tiled=True)
+    returned = pl.pallas_call(
+        giveback_kernel,
+        out_shape=jax.ShapeDtypeStruct((SLOTS, D), BF16),
+        in_specs=[ANY],
+        out_specs=ANY,
+        scratch_shapes=[DMA((PLANE - 1,))] * 2 + [DMA((1,))],
+        compiler_params=remote(3),
+        name="giveback",
+    )(rotated)
     return pl.pallas_call(
         collect_kernel,
         out_shape=jax.ShapeDtypeStruct((ROWS, D), BF16),

time: 456 us -> 311 us (0.68)
  blocking collectives: 170 us -> 0 us
  Pallas kernels: 163 us -> 303 us
  waiting for transfers between devices: 98.2 us -> 0 us
  between operations: 13.4 us -> 0.05 us
    all_to_all x3 -> x0, blocking collectives: 170 us -> none  [the longest x1 79.3 us: body(): lax.all_to_all(rotated, 'bucket', split_axis=0, concat_axis=0, tiled=True)]
    pallas_call x1 -> x4, Pallas kernels: 3.03 us -> 143 us  [the longest x1 48.9 us: body(): pl.pallas_call(giveback_kernel, out_shape=jax.ShapeDtypeStruct((SLOTS, D)...]
    psum x1 -> x0, waiting for transfers between devices: 98.2 us -> none  [body(): reduced = lax.psum(partial, 'replica')]
  transfers between devices with their start and end apart: 1 -> 0, of which waited for: 1 -> 0; matrix products, arithmetic and copies ran while one was open for 0% -> 0% of each run, Pallas kernels for 0% -> 0%
where the time goes in v2:
time: 311 us; the launch traced here: 306 us
  Pallas kernels  303 us (97%)
  local copies, waits for them, and re-layouts  3.75 us (1%)
    pallas_call x1, Pallas kernels, sweeps(): pl.pallas_call(sweeps_kernel, out_shape=[jax.ShapeDtypeStruct((D, D), BF1...  144 us
    pallas_call x1, Pallas kernels, body(): pl.pallas_call(giveback_kernel, out_shape=jax.ShapeDtypeStruct((SLOTS, D)...  48.9 us
    pallas_call x1, Pallas kernels, body(): pl.pallas_call(scatter_kernel, out_shape=[jax.ShapeDtypeStruct((SLOTS, D)...  47.9 us
    pallas_call x1, Pallas kernels, body(): pl.pallas_call(reduce_kernel, out_shape=jax.ShapeDtypeStruct((PACKED, RB)...  43.9 us
    pallas_call x1, Pallas kernels, body(): pl.pallas_call(dispatch_kernel, out_shape=[jax.ShapeDtypeStruct((SLOTS, D...  6.62 us

profile of v2, /device:TPU:26, one launch (start us, length us, event | category | flops | bytes accessed | tf_op | source)
XLA Modules:
  0.0 306.3 jit_solution(4285345236438935593)
XLA Ops:
  0.0 0.0 copy-start.1
  0.0 1.4 copy-done.1
  1.4 0.0 copy-start.2
  1.4 0.7 copy-done.2
  2.1 6.6 %dispatch.1 = (bf16[2048,768]{1,0:T(8,128)(2,1)S(1)}, f32[128,128]{1,0:T(8,128)S(1)}, s32[1024,128]{1,0:T(8,128)S(1)}) custom-call(s32[1,1024]{1,0:T(1,128)S(1)} %bitcast.3, bf16[1024,768]{1,0:T(8,128)(2,1)S(1)} %copy-done.1), custom_call_target="tpu_custom_call" | custom-call | tf_op jit(solution)/shard_map/dispatch/pallas_call | solution.py:486
  8.7 0.0 copy-start
  8.7 1.7 copy-done
  10.4 47.9 %scatter.1 = (bf16[2048,768]{1,0:T(8,128)(2,1)S(1)}, f32[128,128]{1,0:T(8,128)S(1)}, f32[768,768]{1,0:T(8,128)S(1)}) custom-call(bf16[2048,768]{1,0:T(8,128)(2,1)S(1)} %get-tuple-element.13.buffer_ref, f32[128,128]{1,0:T(8,128)S(1)} %get-tuple-element.14.counts_ref, f32[768,768]{1,0:T(8,128)S(1)} %bitcast.2), custom_call_target="tpu_custom_call" | custom-call | tf_op jit(solution)/shard_map/scatter/pallas_call | solution.py:498
  58.3 2.3 moments.1.part_ref
  60.6 43.9 %reduce.1.reduced_ref = f32[2816,128]{1,0:T(8,128)S(1)} custom-call(f32[2816,128]{1,0:T(8,128)S(1)} %moments.1.part_ref), custom_call_target="tpu_custom_call" | custom-call | tf_op jit(solution)/shard_map/reduce/pallas_call | solution.py:519
  104.5 143.7 %sweeps.1 = (bf16[768,768]{1,0:T(8,128)(2,1)S(1)}, f32[8,768]{1,0:T(8,128)S(1)}) custom-call(f32[2816,128]{1,0:T(8,128)S(1)} %reduce.1.reduced_ref, f32[768,768]{1,0:T(8,128)S(1)} %get-tuple-element.17.start_ref), custom_call_target="tpu_custom_call" | custom-call | tf_op jit(solution)/shard_map/sweeps/pallas_call | solution.py:461
  248.2 4.1 %rotate.1.rotated_ref = bf16[2048,768]{1,0:T(8,128)(2,1)S(1)} custom-call(bf16[2048,768]{1,0:T(8,128)(2,1)S(1)} %get-tuple-element.15.received_ref, bf16[768,768]{1,0:T(8,128)(2,1)S(1)} %get-tuple-element.18.w_ref, f32[8,768]{1,0:T(8,128)S(1)} %get-tuple-element.19.shift_ref), custom_call_target="tpu_custom_call" | custom-call | tf_op jit(solution)/shard_map/rotate/pallas_call | solution.py:535
  252.3 48.9 %giveback.1.returned_ref = bf16[2048,768]{1,0:T(8,128)(2,1)S(1)} custom-call(bf16[2048,768]{1,0:T(8,128)(2,1)S(1)} %rotate.1.rotated_ref), custom_call_target="tpu_custom_call" | custom-call | tf_op jit(solution)/shard_map/giveback/pallas_call | solution.py:543
  301.2 5.1 %collect.1 = bf16[1024,768]{1,0:T(8,128)(2,1)} custom-call(bf16[2048,768]{1,0:T(8,128)(2,1)S(1)} %giveback.1.returned_ref, s32[1024,128]{1,0:T(8,128)S(1)} %get-tuple-element.20.place_ref), custom_call_target="tpu_custom_call" | custom-call | tf_op jit(solution)/shard_map/collect/pallas_call | solution.py:552
Async XLA Ops:
  0.0 1.4 copy-start.1
  1.4 0.7 copy-start.2
  8.7 1.7 copy-start

commit v3 on v2

--- a/solution.py
+++ b/solution.py
@@ -46,6 +46,21 @@
     return lax.dot_general(a, b, NT, preferred_element_type=F32)
 
 
+def side(parts):
+    return jnp.concatenate(parts, axis=1)
+
+
+def pile(parts):
+    return jnp.concatenate(parts, axis=0)
+
+
+def thirds(x):
+    high = x.astype(BF16)
+    left = x - high.astype(F32)
+    middle = left.astype(BF16)
+    return high, middle, (left - middle.astype(F32)).astype(BF16)
+
+
 def halves(x):
     high = x.astype(BF16)
     return high, (x - high.astype(F32)).astype(BF16)
@@ -307,53 +322,79 @@
     shape = (8, RB)
     sub = lax.broadcasted_iota(jnp.int32, shape, 0)
     lane = lax.broadcasted_iota(jnp.int32, shape, 1)
-    a = [a_ref[8 * r : 8 * r + 8, :] for r in range(n)]
-    m = [(lane == sub + 8 * r).astype(F32) for r in range(n)]
+    x = [a_ref[8 * r : 8 * r + 8, :] for r in range(n)]
+
+    def wide(v):
+        return jnp.broadcast_to(v, shape)
+
+    def assemble(v):
+        out = v[0]
+        for j in range(1, 8):
+            out = jnp.where(sub == j, v[j], out)
+        return out
+
     for b in range(n):
-        col = [
-            [jnp.broadcast_to(a[r][:, 8 * b + j : 8 * b + j + 1], shape) for j in range(8)]
-            if r >= b
-            else None
-            for r in range(n)
-        ]
+        near = min(b + 2, n)
+        inside = (lane >= 8 * b) & (lane < 8 * b + 8)
+        col = {
+            r: [wide(x[r][:, 8 * b + j : 8 * b + j + 1]) for j in range(8)] for r in range(b, near)
+        }
         s = [
-            [jnp.broadcast_to(col[b][j][i : i + 1, :], shape) if i >= j else None for j in range(8)]
-            for i in range(8)
+            [wide(col[b][j][i : i + 1, :]) if i >= j else None for j in range(8)] for i in range(8)
         ]
         t = [[None] * 8 for _ in range(8)]
         inverse = [None] * 8
-        for j in range(8):
-            inverse[j] = 1.0 / s[j][j]
-            for i in range(j + 1, 8):
+        for j in range(0, 8, 2):
+            p, q, w = s[j][j], s[j + 1][j], s[j + 1][j + 1]
+            inverse[j] = 1.0 / p
+            t[j + 1][j] = q * inverse[j]
+            both = 1.0 / (p * w - q * q)
+            inverse[j + 1] = p * both
+            for i in range(j + 2, 8):
                 t[i][j] = s[i][j] * inverse[j]
-            for k in range(j + 1, 8):
+                t[i][j + 1] = (s[i][j + 1] * p - s[i][j] * q) * both
+            for k in range(j + 2, 8):
+                g0 = (s[k][j] * w - s[k][j + 1] * q) * both
                 for i in range(k, 8):
-                    s[i][k] = s[i][k] - t[k][j] * s[i][j]
-        low = [[None] * 8 for _ in range(n)]
-        for r in range(b, n):
+                    s[i][k] = s[i][k] - g0 * s[i][j] - t[k][j + 1] * s[i][j + 1]
+            s[j + 1][j + 1] = w - t[j + 1][j] * q
+        low = {}
+        for r in range(b, near):
+            c = list(col[r])
+            low[r] = []
             for j in range(8):
                 for i in range(j + 1, 8):
-                    col[r][i] = col[r][i] - col[r][j] * t[i][j]
-                low[r][j] = col[r][j] * inverse[j]
-        panel, inv_panel = a[b], m[b]
-        rows, inv_rows = [], []
+                    c[i] = c[i] - c[j] * t[i][j]
+                low[r].append(c[j] * inverse[j])
+        panel = jnp.where(inside, (lane == sub + 8 * b).astype(F32), x[b])
+        rows = []
         for j in range(8):
-            rows.append(jnp.broadcast_to(panel[j : j + 1, :], shape))
-            inv_rows.append(jnp.broadcast_to(inv_panel[j : j + 1, :], shape))
+            rows.append(wide(panel[j : j + 1, :]))
             if j < 7:
-                below = jnp.where(sub > j, low[b][j], 0.0)
-                panel = panel - below * rows[j]
-                inv_panel = inv_panel - below * inv_rows[j]
-        pivots = s[0][0]
-        for j in range(1, 8):
-            pivots = jnp.where(sub == j, s[j][j], pivots)
-        m[b] = inv_panel * lax.rsqrt(pivots)
-        for r in range(b + 1, n):
-            for j in range(8):
-                a[r] = a[r] - low[r][j] * rows[j]
-                m[r] = m[r] - low[r][j] * inv_rows[j]
+                panel = panel - jnp.where(sub > j, low[b][j], 0.0) * rows[j]
+        pivots = assemble([s[j][j] for j in range(8)])
+        x[b] = jnp.where(lane < 8 * b + 8, panel * lax.rsqrt(pivots), 0.0)
+        for r in range(b + 1, near):
+            even, odd = low[r][0] * rows[0], low[r][1] * rows[1]
+            for j in range(2, 8, 2):
+                even = even + low[r][j] * rows[j]
+                odd = odd + low[r][j + 1] * rows[j + 1]
+            x[r] = jnp.where(inside, 0.0, x[r]) - (even + odd)
+        if near < n:
+            g = [rows[j] * inverse[j] for j in range(8)]
+            for j in range(7, 0, -1):
+                for i in range(j):
+                    g[i] = g[i] - t[j][i] * g[j]
+            above = [jnp.zeros((8 * b, RB), F32)] if b else []
+            below = [jnp.zeros((RB - 8 * b - 8, RB), F32)]
+            g_high, g_low = halves(jnp.concatenate(above + [assemble(g)] + below, axis=0))
+            x_high, x_low = halves(jnp.concatenate(x[near:], axis=0))
+            change = dot(x_high, g_high) + dot(x_high, g_low) + dot(x_low, g_high)
+            for r in range(near, n):
+                first = 8 * (r - near)
+                x[r] = jnp.where(inside, 0.0, x[r]) - change[first : first + 8, :]
     for r in range(n):
-        m_ref[8 * r : 8 * r + 8, :] = m[r]
+        m_ref[8 * r : 8 * r + 8, :] = x[r]
 
 
 def sweeps_kernel(
@@ -364,13 +405,23 @@
     mean = jnp.concatenate(
         [reduced_ref[TAIL + block : TAIL + block + 1, :] / divisor for block in range(NB)], axis=1
     )
-    first = lax.broadcasted_iota(jnp.int32, (8, D), 0) == 0
-    mean_rows = jnp.where(first, jnp.broadcast_to(mean, (8, D)), 0.0)
+    m1, m2, m3 = thirds(jnp.broadcast_to(mean, (16, D)))
+    row = lax.broadcasted_iota(jnp.int32, (16, D), 0)
+    nothing = jnp.zeros((16, D), F32)
+    m1, m2, m3 = m1.astype(F32), m2.astype(F32), m3.astype(F32)
+
+    def stack(parts):
+        out = nothing
+        for index, part in enumerate(parts):
+            out = jnp.where(row == index, part, out)
+        return out.astype(BF16)
+
+    mean_left = stack([m1, m1, m2, m1, m3, m2])
+    mean_right = stack([m1, m2, m1, m3, m1, m2])
     for block in range(NB):
         span = slice(block * RB, block * RB + RB)
         outer = lax.dot_general(
-            mean_rows[:, span], mean_rows, TN, preferred_element_type=F32,
-            precision=lax.Precision.HIGHEST,
+            mean_left[:, span], mean_right, TN, preferred_element_type=F32,
         )
         for other in range(NB):
             columns = slice(other * RB, other * RB + RB)
@@ -388,49 +439,75 @@
     def sweep(step, carry):
         for block in range(D // 256):
             span = slice(block * 256, block * 256 + 256)
-            image = (
-                dot(w_high[span, :], c_high[...])
-                + dot(w_high[span, :], c_low[...])
-                + dot(w_low[span, :], c_high[...])
-            )
+            high, low = w_high[span, :], w_low[span, :]
+            image = dot(side([high, high, low]), pile([c_high[...], c_low[...], c_high[...]]))
             y[span, :] = image
             high, low = halves(image)
             y_high[span, :] = high
             y_low[span, :] = low
 
+        last = step == SWEEPS - 1
+
         def block_step(block, inner):
             span = pl.ds(pl.multiple_of(block * RB, RB), RB)
-            high, low = y_high[span, :], y_low[span, :]
-            gram[...] = dot_nt(high, high) + dot_nt(high, low) + dot_nt(low, high)
+
+            @pl.when(jnp.logical_not(last))
+            def _():
+                gram[...] = dot_nt(y_high[span, :], y_high[span, :])
+
+            @pl.when(last)
+            def _():
+                high, low = y_high[span, :], y_low[span, :]
+                gram[...] = dot_nt(side([high, high, low]), side([high, low, high]))
+
             factor(gram, inverse)
             i_high, i_low = halves(inverse[...])
-            w_h, w_l = halves(dot(i_high, high) + dot(i_high, low) + dot(i_low, high))
-            w_high[span, :] = w_h
-            w_low[span, :] = w_l
+
+            def keep(own):
+                high, low = halves(own)
+                w_high[span, :] = high
+                w_low[span, :] = low
+
+            @pl.when(jnp.logical_not(last))
+            def _():
+                keep(dot(side([i_high, i_high]), pile([y_high[span, :], y_low[span, :]])))
+
+            @pl.when(last)
+            def _():
+                high, low = y_high[span, :], y_low[span, :]
+                keep(dot(side([i_high, i_high, i_low]), pile([high, low, high])))
+
             for done in range(NB - 1):
-
-                @pl.when(block == done)
-                def _():
-                    rest = slice(RB * (done + 1), D)
-                    own = slice(RB * done, RB * done + RB)
-                    u_h, u_l = w_high[own, :], w_low[own, :]
-                    r_h, r_l = y_high[rest, :], y_low[rest, :]
-                    l_h, l_l = halves(dot_nt(r_h, u_h) + dot_nt(r_h, u_l) + dot_nt(r_l, u_h))
-                    left = y[rest, :] - (dot(l_h, u_h) + dot(l_h, u_l) + dot(l_l, u_h))
+                rest = slice(RB * (done + 1), D)
+                own = slice(RB * done, RB * done + RB)
+
+                def remove(change, rest=rest):
+                    left = y[rest, :] - change
                     y[rest, :] = left
                     high, low = halves(left)
                     y_high[rest, :] = high
                     y_low[rest, :] = low
 
+                @pl.when((block == done) & jnp.logical_not(last))
+                def _(rest=rest, own=own, remove=remove):
+                    u_h, u_l = w_high[own, :], w_low[own, :]
+                    l_h = dot_nt(y_high[rest, :], u_h).astype(BF16)
+                    remove(dot(side([l_h, l_h]), pile([u_h, u_l])))
+
+                @pl.when((block == done) & last)
+                def _(rest=rest, own=own, remove=remove):
+                    u_h, u_l = w_high[own, :], w_low[own, :]
+                    r_h, r_l = y_high[rest, :], y_low[rest, :]
+                    l_h, l_l = halves(dot_nt(side([r_h, r_h, r_l]), side([u_h, u_l, u_h])))
+                    remove(dot(side([l_h, l_h, l_l]), pile([u_h, u_l, u_h])))
+
             return inner
 
         return lax.fori_loop(0, NB, block_step, carry)
 
     lax.fori_loop(0, SWEEPS, sweep, 0)
-    shift_ref[...] = lax.dot_general(
-        jnp.broadcast_to(mean, (8, D)), w_high[...].astype(F32), NT,
-        preferred_element_type=F32, precision=lax.Precision.HIGHEST,
-    )
+    shifts = dot_nt(stack([m1, m2, m3]), w_high[...])
+    shift_ref[...] = jnp.broadcast_to(shifts[0:1, :] + shifts[1:2, :] + shifts[2:3, :], (8, D))
 
 
 def rotate_kernel(received_ref, w_ref, shift_ref, out_ref):

time: 311 us -> 268 us (0.86)
  Pallas kernels: 303 us -> 260 us
    pallas_call x1, Pallas kernels: 144 us -> 101 us  [sweeps(): pl.pallas_call(sweeps_kernel, out_shape=[jax.ShapeDtypeStruct((D, D), BF1...]
where the time goes in v3:
time: 268 us; the launch traced here: 264 us
  Pallas kernels  260 us (97%)
  local copies, waits for them, and re-layouts  3.75 us (1%)
    pallas_call x1, Pallas kernels, sweeps(): pl.pallas_call(sweeps_kernel, out_shape=[jax.ShapeDtypeStruct((D, D), BF1...  101 us
    pallas_call x1, Pallas kernels, body(): pl.pallas_call(giveback_kernel, out_shape=jax.ShapeDtypeStruct((SLOTS, D)...  49 us
    pallas_call x1, Pallas kernels, body(): pl.pallas_call(scatter_kernel, out_shape=[jax.ShapeDtypeStruct((SLOTS, D)...  47.9 us
    pallas_call x1, Pallas kernels, body(): pl.pallas_call(reduce_kernel, out_shape=jax.ShapeDtypeStruct((PACKED, RB)...  43.9 us
    pallas_call x1, Pallas kernels, body(): pl.pallas_call(dispatch_kernel, out_shape=[jax.ShapeDtypeStruct((SLOTS, D...  6.62 us

profile of v3, /device:TPU:26, one launch (start us, length us, event | category | flops | bytes accessed | tf_op | source)
XLA Modules:
  0.0 263.9 jit_solution(5645149241606340523)
XLA Ops:
  0.0 0.0 copy-start.1
  0.0 1.4 copy-done.1
  1.4 0.0 copy-start.2
  1.4 0.7 copy-done.2
  2.1 6.6 %dispatch.1 = (bf16[2048,768]{1,0:T(8,128)(2,1)S(1)}, f32[128,128]{1,0:T(8,128)S(1)}, s32[1024,128]{1,0:T(8,128)S(1)}) custom-call(s32[1,1024]{1,0:T(1,128)S(1)} %bitcast.3, bf16[1024,768]{1,0:T(8,128)(2,1)S(1)} %copy-done.1), custom_call_target="tpu_custom_call" | custom-call | tf_op jit(solution)/shard_map/dispatch/pallas_call | solution.py:563
  8.7 0.0 copy-start
  8.7 1.7 copy-done
  10.4 47.9 %scatter.1 = (bf16[2048,768]{1,0:T(8,128)(2,1)S(1)}, f32[128,128]{1,0:T(8,128)S(1)}, f32[768,768]{1,0:T(8,128)S(1)}) custom-call(bf16[2048,768]{1,0:T(8,128)(2,1)S(1)} %get-tuple-element.13.buffer_ref, f32[128,128]{1,0:T(8,128)S(1)} %get-tuple-element.14.counts_ref, f32[768,768]{1,0:T(8,128)S(1)} %bitcast.2), custom_call_target="tpu_custom_call" | custom-call | tf_op jit(solution)/shard_map/scatter/pallas_call | solution.py:575
  58.3 2.3 moments.1.part_ref
  60.6 43.9 %reduce.1.reduced_ref = f32[2816,128]{1,0:T(8,128)S(1)} custom-call(f32[2816,128]{1,0:T(8,128)S(1)} %moments.1.part_ref), custom_call_target="tpu_custom_call" | custom-call | tf_op jit(solution)/shard_map/reduce/pallas_call | solution.py:596
  104.5 101.2 %sweeps.1 = (bf16[768,768]{1,0:T(8,128)(2,1)S(1)}, f32[8,768]{1,0:T(8,128)S(1)}) custom-call(f32[2816,128]{1,0:T(8,128)S(1)} %reduce.1.reduced_ref, f32[768,768]{1,0:T(8,128)S(1)} %get-tuple-element.17.start_ref), custom_call_target="tpu_custom_call" | custom-call | tf_op jit(solution)/shard_map/sweeps/pallas_call | solution.py:538
  205.7 4.1 %rotate.1.rotated_ref = bf16[2048,768]{1,0:T(8,128)(2,1)S(1)} custom-call(bf16[2048,768]{1,0:T(8,128)(2,1)S(1)} %get-tuple-element.15.received_ref, bf16[768,768]{1,0:T(8,128)(2,1)S(1)} %get-tuple-element.18.w_ref, f32[8,768]{1,0:T(8,128)S(1)} %get-tuple-element.19.shift_ref), custom_call_target="tpu_custom_call" | custom-call | tf_op jit(solution)/shard_map/rotate/pallas_call | solution.py:612
  209.9 49.0 %giveback.1.returned_ref = bf16[2048,768]{1,0:T(8,128)(2,1)S(1)} custom-call(bf16[2048,768]{1,0:T(8,128)(2,1)S(1)} %rotate.1.rotated_ref), custom_call_target="tpu_custom_call" | custom-call | tf_op jit(solution)/shard_map/giveback/pallas_call | solution.py:620
  258.9 5.1 %collect.1 = bf16[1024,768]{1,0:T(8,128)(2,1)} custom-call(bf16[2048,768]{1,0:T(8,128)(2,1)S(1)} %giveback.1.returned_ref, s32[1024,128]{1,0:T(8,128)S(1)} %get-tuple-element.20.place_ref), custom_call_target="tpu_custom_call" | custom-call | tf_op jit(solution)/shard_map/collect/pallas_call | solution.py:629
Async XLA Ops:
  0.0 1.4 copy-start.1
  1.4 0.7 copy-start.2
  8.7 1.7 copy-start

commit v4 on v3

--- a/solution.py
+++ b/solution.py
@@ -31,6 +31,10 @@
 PACKED = 2 * HALF
 TAIL = len(PAIRS) * RB
 PIECES = 12
+ORDER = (
+    (0, 1), (2, 2), (1, 0), (1, 2), (0, 3), (2, 1), (3, 0), (2, 3),
+    (1, 1), (0, 2), (3, 3), (2, 0), (1, 3), (3, 2), (3, 1),
+)
 PIECE = D // PIECES
 
 
@@ -66,7 +70,48 @@
     return high, (x - high.astype(F32)).astype(BF16)
 
 
-def dispatch_kernel(ids_ref, rows_ref, buffer_ref, counts_ref, place_ref):
+def scatter_kernel(
+    ids_ref, rows_ref, basis_ref, received_ref, got_counts_ref, got_basis_ref, place_ref,
+    buffer, counts,
+    send, recv, send_count, recv_count, send_up, send_down, send_across, recv_chain, recv_across, own
+):
+    bucket, me = lax.axis_index("bucket"), lax.axis_index("replica")
+    z, core = bucket // 2, bucket % 2
+    origin, chain_core = me // 2, me % 2
+    away = lax.rem(z + RING - origin, RING)
+    up = lax.rem(z + 1, RING) * 2 + core
+    down = lax.rem(z + RING - 1, RING) * 2 + core
+    across = z * 2 + (1 - core)
+    peers = plane_peers(me)
+
+    barrier = pltpu.get_barrier_semaphore()
+    for peer in peers:
+        pl.semaphore_signal(barrier, inc=1, device_id=(bucket, peer), device_id_type=MESH)
+    for other in (up, down, across):
+        pl.semaphore_signal(barrier, inc=1, device_id=(other, me), device_id_type=MESH)
+    pl.semaphore_wait(barrier, len(peers) + 3)
+
+    def passing(source, index, sends, receives, target):
+        span = pl.ds(index * PIECE, PIECE)
+        return pltpu.make_async_remote_copy(
+            source.at[span], got_basis_ref.at[span], sends.at[index], receives.at[index],
+            device_id=(target, me), device_id_type=MESH,
+        )
+
+    on_chain = core == chain_core
+    first = on_chain & (away == 0)
+    later = on_chain & (away > 0)
+
+    whole = pltpu.make_async_copy(basis_ref, got_basis_ref, own.at[2])
+
+    @pl.when(first)
+    def _():
+        for index in range(PIECES):
+            passing(basis_ref, index, send_up, recv_chain, up).start()
+            passing(basis_ref, index, send_down, recv_chain, down).start()
+            passing(basis_ref, index, send_across, recv_across, across).start()
+        whole.start()
+
     ids = ids_ref[...]
     cells = lax.broadcasted_iota(jnp.int32, (CELLS, ROWS), 0)
     onehot = (ids == cells).astype(F32)
@@ -79,77 +124,39 @@
     place = ids * CAP + slot
     eighth = lax.broadcasted_iota(jnp.int32, (8 * CELLS, ROWS), 0) // 8
     each = jnp.sum((ids == eighth).astype(F32), axis=1, keepdims=True)
-    counts_ref[...] = jnp.broadcast_to(each, (8 * CELLS, 128))
-    place_ref[...] = jnp.broadcast_to(place, (128, ROWS)).T
-
-    def fill(cell, carry):
+    counts[...] = jnp.broadcast_to(each, (8 * CELLS, 128))
+
+    def fill(cell):
         wanted = lax.broadcasted_iota(jnp.int32, (CAP, ROWS), 0) + cell * CAP
         pick = (place == wanted).astype(F32).astype(BF16)
-        first = pl.multiple_of(cell * CAP, CAP)
-        buffer_ref[pl.ds(first, CAP), :] = dot(pick, rows_ref[...]).astype(BF16)
-        return carry
-
-    lax.fori_loop(0, CELLS, fill, 0)
-
-
-def scatter_kernel(
-    buffer_ref, counts_ref, basis_ref, received_ref, got_counts_ref, got_basis_ref,
-    send, recv, send_count, recv_count, send_up, send_down, send_across, recv_chain, recv_across, own
-):
-    bucket, me = lax.axis_index("bucket"), lax.axis_index("replica")
-    z, core = bucket // 2, bucket % 2
-    origin, chain_core = me // 2, me % 2
-    away = lax.rem(z + RING - origin, RING)
-    up = lax.rem(z + 1, RING) * 2 + core
-    down = lax.rem(z + RING - 1, RING) * 2 + core
-    across = z * 2 + (1 - core)
-    peers = plane_peers(me)
-
-    barrier = pltpu.get_barrier_semaphore()
-    for peer in peers:
-        pl.semaphore_signal(barrier, inc=1, device_id=(bucket, peer), device_id_type=MESH)
-    for other in (up, down, across):
-        pl.semaphore_signal(barrier, inc=1, device_id=(other, me), device_id_type=MESH)
-    pl.semaphore_wait(barrier, len(peers) + 3)
+        start = pl.multiple_of(cell * CAP, CAP)
+        buffer[pl.ds(start, CAP), :] = dot(pick, rows_ref[...]).astype(BF16)
 
     copies = []
     for index, peer in enumerate(peers):
+        fill(peer)
+        copies.append(exchange(buffer, received_ref, send, recv, index, bucket, me, peer))
+        copies[-1].start()
+    fill(me)
+    for index, peer in enumerate(peers):
         copies.append(pltpu.make_async_remote_copy(
-            counts_ref.at[pl.ds(pl.multiple_of(peer * 8, 8), 8)],
+            counts.at[pl.ds(pl.multiple_of(peer * 8, 8), 8)],
             got_counts_ref.at[pl.ds(pl.multiple_of(me * 8, 8), 8)],
             send_count.at[index], recv_count.at[index], device_id=(bucket, peer), device_id_type=MESH,
         ))
-        copies.append(exchange(buffer_ref, received_ref, send, recv, index, bucket, me, peer))
-    for copy in copies:
-        copy.start()
+        copies[-1].start()
     mine = pl.ds(pl.multiple_of(me * CAP, CAP), CAP)
     mine_counts = pl.ds(pl.multiple_of(me * 8, 8), 8)
     local = [
-        pltpu.make_async_copy(buffer_ref.at[mine], received_ref.at[mine], own.at[0]),
-        pltpu.make_async_copy(counts_ref.at[mine_counts], got_counts_ref.at[mine_counts], own.at[1]),
+        pltpu.make_async_copy(buffer.at[mine], received_ref.at[mine], own.at[0]),
+        pltpu.make_async_copy(counts.at[mine_counts], got_counts_ref.at[mine_counts], own.at[1]),
     ]
     for copy in local:
         copy.start()
-
-    def passing(source, index, sends, receives, target):
-        span = pl.ds(index * PIECE, PIECE)
-        return pltpu.make_async_remote_copy(
-            source.at[span], got_basis_ref.at[span], sends.at[index], receives.at[index],
-            device_id=(target, me), device_id_type=MESH,
-        )
-
-    on_chain = core == chain_core
-    first = on_chain & (away == 0)
-    later = on_chain & (away > 0)
+    place_ref[...] = jnp.broadcast_to(place, (128, ROWS)).T
 
     @pl.when(first)
     def _():
-        whole = pltpu.make_async_copy(basis_ref, got_basis_ref, own.at[2])
-        whole.start()
-        for index in range(PIECES):
-            passing(basis_ref, index, send_up, recv_chain, up).start()
-            passing(basis_ref, index, send_down, recv_chain, down).start()
-            passing(basis_ref, index, send_across, recv_across, across).start()
         for index in range(PIECES):
             passing(basis_ref, index, send_up, recv_chain, up).wait_send()
             passing(basis_ref, index, send_down, recv_chain, down).wait_send()
@@ -196,10 +203,7 @@
     y, x = me // 4, me % 4
     return [
         lax.rem(y + dy, 4) * 4 + lax.rem(x + dx, 4)
-        for dy, dx in sorted(
-            ((dy, dx) for dy in range(4) for dx in range(4) if dy or dx),
-            key=lambda o: -min(o[0], 4 - o[0]) - min(o[1], 4 - o[1]),
-        )
+        for dy, dx in ORDER
     ]
 
 
@@ -211,21 +215,34 @@
     )
 
 
-def giveback_kernel(rotated_ref, returned_ref, send, recv, own):
+def giveback_kernel(received_ref, w_ref, shift_ref, returned_ref, rotated, send, recv, own):
     bucket, me = lax.axis_index("bucket"), lax.axis_index("replica")
     peers = plane_peers(me)
     barrier = pltpu.get_barrier_semaphore()
     for peer in peers:
         pl.semaphore_signal(barrier, inc=1, device_id=(bucket, peer), device_id_type=MESH)
     pl.semaphore_wait(barrier, len(peers))
-    copies = [
-        exchange(rotated_ref, returned_ref, send, recv, index, bucket, me, peer)
-        for index, peer in enumerate(peers)
-    ]
-    mine = pl.ds(pl.multiple_of(me * CAP, CAP), CAP)
-    copies.append(pltpu.make_async_copy(rotated_ref.at[mine], returned_ref.at[mine], own.at[0]))
-    for copy in copies:
-        copy.start()
+
+    def block(peer):
+        return pl.ds(pl.multiple_of(peer * CAP, CAP), CAP)
+
+    copies = []
+    order = peers + [me]
+    for index in range(0, PLANE, 2):
+        pair = order[index : index + 2]
+        product = dot_nt(pile([received_ref[block(peer), :] for peer in pair]), w_ref[...])
+        values = (product - shift_ref[0:1, :]).astype(BF16)
+        for half, peer in enumerate(pair):
+            rotated[block(peer), :] = values[half * CAP : half * CAP + CAP, :]
+            if index + half < PLANE - 1:
+                copies.append(
+                    exchange(rotated, returned_ref, send, recv, index + half, bucket, me, peer)
+                )
+            else:
+                copies.append(
+                    pltpu.make_async_copy(rotated.at[block(me)], returned_ref.at[block(me)], own.at[0])
+                )
+            copies[-1].start()
     for copy in copies:
         copy.wait()
 
@@ -262,25 +279,34 @@
         pl.semaphore_signal(barrier, inc=1, device_id=other, device_id_type=MESH)
     pl.semaphore_wait(barrier, RING)
 
-    half = pltpu.make_async_remote_copy(
-        part_ref.at[pl.ds(pl.multiple_of((1 - core) * HALF, 8), HALF)], arrived,
-        send_half, recv_half, device_id=across, device_id_type=MESH,
-    )
-    half.start()
-    half.wait()
-    mine[...] = part_ref[pl.ds(pl.multiple_of(core * HALF, 8), HALF), :] + arrived[...]
-
-    order = [4, 3, 5, 2, 6, 1, 7]
+    def rows_of(chunk):
+        return pl.ds(pl.multiple_of(chunk * CHUNK, 8), CHUNK)
+
+    order = [1, 7, 2, 6, 3, 5, 4]
+    halves_out = {}
+    for step in order + [0]:
+        chunk = lax.rem(z + step, RING)
+        halves_out[step] = pltpu.make_async_remote_copy(
+            part_ref.at[rows_of((1 - core) * RING + chunk)], arrived.at[rows_of(chunk)],
+            send_half.at[step], recv_half.at[step], device_id=across, device_id_type=MESH,
+        )
+        halves_out[step].start()
+
+    def add_pair(step):
+        chunk = lax.rem(z + step, RING)
+        halves_out[step].wait_recv()
+        mine[rows_of(chunk), :] = part_ref[rows_of(core * RING + chunk), :] + arrived[rows_of(chunk), :]
+
     parts = []
     for step in order:
-        chunk = lax.rem(z + step, RING)
+        add_pair(step)
         parts.append(pltpu.make_async_remote_copy(
-            mine.at[pl.ds(pl.multiple_of(chunk * CHUNK, 8), CHUNK)], slots.at[step],
+            mine.at[rows_of(lax.rem(z + step, RING))], slots.at[step],
             send_part.at[step], recv_part.at[step], device_id=ring[step], device_id_type=MESH,
         ))
-    for copy in parts:
-        copy.start()
-    total = mine[pl.ds(pl.multiple_of(z * CHUNK, 8), CHUNK), :]
+        parts[-1].start()
+    add_pair(0)
+    total = mine[rows_of(z), :]
     for step, copy in zip(order, parts):
         copy.wait_recv()
         total = total + slots[step]
@@ -312,7 +338,7 @@
         forward(step).start()
     for step in range(RING):
         forward(step).wait()
-    for copy in parts + spread:
+    for copy in parts + spread + list(halves_out.values()):
         copy.wait_send()
     out_ref[...] = full[...]
 
@@ -510,16 +536,6 @@
     shift_ref[...] = jnp.broadcast_to(shifts[0:1, :] + shifts[1:2, :] + shifts[2:3, :], (8, D))
 
 
-def rotate_kernel(received_ref, w_ref, shift_ref, out_ref):
-    def step(index, carry):
-        span = pl.ds(pl.multiple_of(index * 256, 256), 256)
-        product = dot_nt(received_ref[span, :], w_ref[...])
-        out_ref[span, :] = (product - shift_ref[0:1, :]).astype(BF16)
-        return carry
-
-    lax.fori_loop(0, SLOTS // 256, step, 0)
-
-
 def collect_kernel(returned_ref, place_ref, out_ref):
     def step(index, carry):
         span = pl.ds(pl.multiple_of(index * 256, 256), 256)
@@ -560,31 +576,21 @@
 
 
 def body(rows, cell_ids, start_basis):
-    buffer, counts, place = pl.pallas_call(
-        dispatch_kernel,
-        out_shape=[
-            jax.ShapeDtypeStruct((SLOTS, D), BF16),
-            jax.ShapeDtypeStruct((8 * CELLS, 128), F32),
-            jax.ShapeDtypeStruct((ROWS, 128), jnp.int32),
-        ],
-        in_specs=[VMEM, VMEM],
-        out_specs=[VMEM] * 3,
-        compiler_params=params(40),
-        name="dispatch",
-    )(cell_ids.reshape(1, ROWS), rows)
-    received, got_counts, basis = pl.pallas_call(
+    received, got_counts, basis, place = pl.pallas_call(
         scatter_kernel,
         out_shape=[
             jax.ShapeDtypeStruct((SLOTS, D), BF16),
             jax.ShapeDtypeStruct((8 * CELLS, 128), F32),
             jax.ShapeDtypeStruct((D, D), F32),
+            jax.ShapeDtypeStruct((ROWS, 128), jnp.int32),
         ],
-        in_specs=[ANY] * 3,
-        out_specs=[ANY] * 3,
-        scratch_shapes=[DMA((PLANE - 1,))] * 4 + [DMA((PIECES,))] * 5 + [DMA((3,))],
+        in_specs=[VMEM, VMEM, ANY],
+        out_specs=[ANY] * 3 + [VMEM],
+        scratch_shapes=[pltpu.VMEM((SLOTS, D), BF16), pltpu.VMEM((8 * CELLS, 128), F32)]
+        + [DMA((PLANE - 1,))] * 4 + [DMA((PIECES,))] * 5 + [DMA((3,))],
         compiler_params=remote(1),
         name="scatter",
-    )(buffer, counts, start_basis[0])
+    )(cell_ids.reshape(1, ROWS), rows, start_basis[0])
     partial = pl.pallas_call(
         moments_kernel,
         out_shape=jax.ShapeDtypeStruct((PACKED, RB), F32),
@@ -603,29 +609,20 @@
             pltpu.VMEM((HALF, RB), F32),
             pltpu.VMEM((HALF, RB), F32),
             pltpu.VMEM((RING, CHUNK, RB), F32),
-            DMA, DMA,
-        ] + [DMA((RING,))] * 6,
+        ] + [DMA((RING,))] * 8,
         compiler_params=remote(2),
         name="reduce",
     )(partial)
     rotation, shift = sweeps(reduced, basis)
-    rotated = pl.pallas_call(
-        rotate_kernel,
-        out_shape=jax.ShapeDtypeStruct((SLOTS, D), BF16),
-        in_specs=[VMEM] * 3,
-        out_specs=VMEM,
-        compiler_params=params(40),
-        name="rotate",
-    )(received, rotation, shift)
     returned = pl.pallas_call(
         giveback_kernel,
         out_shape=jax.ShapeDtypeStruct((SLOTS, D), BF16),
-        in_specs=[ANY],
+        in_specs=[VMEM] * 3,
         out_specs=ANY,
-        scratch_shapes=[DMA((PLANE - 1,))] * 2 + [DMA((1,))],
+        scratch_shapes=[pltpu.VMEM((SLOTS, D), BF16)] + [DMA((PLANE - 1,))] * 2 + [DMA((1,))],
         compiler_params=remote(3),
         name="giveback",
-    )(rotated)
+    )(received, rotation, shift)
     return pl.pallas_call(
         collect_kernel,
         out_shape=jax.ShapeDtypeStruct((ROWS, D), BF16),

time: 268 us -> 260 us (0.970); the launches traced: 264 us -> 260 us
  Pallas kernels: 260 us -> 256 us
    pallas_call x2 -> x0, Pallas kernels: 10.7 us -> none  [the longest x1 6.62 us: body(): pl.pallas_call(dispatch_kernel, out_shape=[jax.ShapeDtypeStruct((SLOTS, D...]
where the time goes in v4:
time: 260 us
  Pallas kernels  256 us (98%)
  local copies, waits for them, and re-layouts  3.76 us (1%)
    pallas_call x1, Pallas kernels, sweeps(): pl.pallas_call(sweeps_kernel, out_shape=[jax.ShapeDtypeStruct((D, D), BF1...  101 us
    pallas_call x1, Pallas kernels, body(): pl.pallas_call(giveback_kernel, out_shape=jax.ShapeDtypeStruct((SLOTS, D)...  51 us
    pallas_call x1, Pallas kernels, body(): pl.pallas_call(scatter_kernel, out_shape=[jax.ShapeDtypeStruct((SLOTS, D)...  50.4 us
    pallas_call x1, Pallas kernels, body(): pl.pallas_call(reduce_kernel, out_shape=jax.ShapeDtypeStruct((PACKED, RB)...  46 us

profile of v4, /device:TPU:26, one launch (start us, length us, event | category | flops | bytes accessed | tf_op | source)
XLA Modules:
  0.0 260.1 jit_solution(17747547081284416460)
XLA Ops:
  0.0 0.0 copy-start
  0.0 1.7 copy-done
  1.7 0.0 copy-start.1
  1.7 1.4 copy-done.1
  3.1 0.0 copy-start.2
  3.1 0.7 copy-done.2
  3.8 50.4 %scatter.1 = (bf16[2048,768]{1,0:T(8,128)(2,1)S(1)}, f32[128,128]{1,0:T(8,128)S(1)}, f32[768,768]{1,0:T(8,128)S(1)}, s32[1024,128]{1,0:T(8,128)S(1)}) custom-call(s32[1,1024]{1,0:T(1,128)S(1)} %bitcast.3, bf16[1024,768]{1,0:T(8,128)(2,1)S(1)} %copy-done.1, f32[768,768]{1,0:T(8,128)S(1)} %bitcast.2), custom_call_target="tpu_custom_call" | custom-call | tf_op jit(solution)/shard_map/scatter/pallas_call | solution.py:579
  54.2 2.3 moments.1.part_ref
  56.4 46.0 %reduce.1.reduced_ref = f32[2816,128]{1,0:T(8,128)S(1)} custom-call(f32[2816,128]{1,0:T(8,128)S(1)} %moments.1.part_ref), custom_call_target="tpu_custom_call" | custom-call | tf_op jit(solution)/shard_map/reduce/pallas_call | solution.py:602
  102.5 101.4 %sweeps.1 = (bf16[768,768]{1,0:T(8,128)(2,1)S(1)}, f32[8,768]{1,0:T(8,128)S(1)}) custom-call(f32[2816,128]{1,0:T(8,128)S(1)} %reduce.1.reduced_ref, f32[768,768]{1,0:T(8,128)S(1)} %get-tuple-element.13.start_ref), custom_call_target="tpu_custom_call" | custom-call | tf_op jit(solution)/shard_map/sweeps/pallas_call | solution.py:554
  203.9 51.0 %giveback.1.returned_ref = bf16[2048,768]{1,0:T(8,128)(2,1)S(1)} custom-call(bf16[2048,768]{1,0:T(8,128)(2,1)S(1)} %get-tuple-element.11.received_ref, bf16[768,768]{1,0:T(8,128)(2,1)S(1)} %get-tuple-element.14.w_ref, f32[8,768]{1,0:T(8,128)S(1)} %get-tuple-element.15.shift_ref), custom_call_target="tpu_custom_call" | custom-call | tf_op jit(solution)/shard_map/giveback/pallas_call | solution.py:617
  254.9 5.2 %collect.1 = bf16[1024,768]{1,0:T(8,128)(2,1)} custom-call(bf16[2048,768]{1,0:T(8,128)(2,1)S(1)} %giveback.1.returned_ref, s32[1024,128]{1,0:T(8,128)S(1)} %get-tuple-element.16.place_ref), custom_call_target="tpu_custom_call" | custom-call | tf_op jit(solution)/shard_map/collect/pallas_call | solution.py:626
Async XLA Ops:
  0.0 1.7 copy-start
  1.7 1.4 copy-start.1
  3.1 0.7 copy-start.2

commit v5 on v4

--- a/solution.py
+++ b/solution.py
@@ -343,7 +343,7 @@
     out_ref[...] = full[...]
 
 
-def factor(a_ref, m_ref):
+def factor(a_ref, m_ref, columns):
     n = RB // 8
     shape = (8, RB)
     sub = lax.broadcasted_iota(jnp.int32, shape, 0)
@@ -365,8 +365,12 @@
         col = {
             r: [wide(x[r][:, 8 * b + j : 8 * b + j + 1]) for j in range(8)] for r in range(b, near)
         }
+        base = 64 * (b % 2)
+        for j in range(8):
+            columns[base + 8 * j : base + 8 * j + 8, :] = col[b][j]
         s = [
-            [wide(col[b][j][i : i + 1, :]) if i >= j else None for j in range(8)] for i in range(8)
+            [columns[pl.ds(base + 8 * j + i, 8, stride=0), :] if i >= j else None for j in range(8)]
+            for i in range(8)
         ]
         t = [[None] * 8 for _ in range(8)]
         inverse = [None] * 8
@@ -415,7 +419,8 @@
             below = [jnp.zeros((RB - 8 * b - 8, RB), F32)]
             g_high, g_low = halves(jnp.concatenate(above + [assemble(g)] + below, axis=0))
             x_high, x_low = halves(jnp.concatenate(x[near:], axis=0))
-            change = dot(x_high, g_high) + dot(x_high, g_low) + dot(x_low, g_high)
+            two = dot(x_high, side([g_high, g_low]))
+            change = two[:, :RB] + two[:, RB:] + dot(x_low, g_high)
             for r in range(near, n):
                 first = 8 * (r - near)
                 x[r] = jnp.where(inside, 0.0, x[r]) - change[first : first + 8, :]
@@ -424,7 +429,7 @@
 
 
 def sweeps_kernel(
-    reduced_ref, start_ref, w_high, shift_ref, c_high, c_low, y, y_high, y_low, w_low, gram, inverse
+    reduced_ref, start_ref, w_high, shift_ref, c_high, c_low, y, y_high, y_low, w_low, gram, inverse, spread_columns
 ):
     count = reduced_ref[TAIL + NB : TAIL + NB + 1, :]
     divisor = jnp.maximum(count, 1.0)
@@ -471,62 +476,52 @@
             high, low = halves(image)
             y_high[span, :] = high
             y_low[span, :] = low
+            if block == 0:
+                high, low = high[:RB, :], low[:RB, :]
+                gram[...] = dot_nt(side([high, high, low]), side([high, low, high]))
 
         last = step == SWEEPS - 1
 
         def block_step(block, inner):
-            span = pl.ds(pl.multiple_of(block * RB, RB), RB)
-
-            @pl.when(jnp.logical_not(last))
-            def _():
-                gram[...] = dot_nt(y_high[span, :], y_high[span, :])
-
-            @pl.when(last)
-            def _():
-                high, low = y_high[span, :], y_low[span, :]
-                gram[...] = dot_nt(side([high, high, low]), side([high, low, high]))
-
-            factor(gram, inverse)
-            i_high, i_low = halves(inverse[...])
-
-            def keep(own):
-                high, low = halves(own)
-                w_high[span, :] = high
-                w_low[span, :] = low
-
-            @pl.when(jnp.logical_not(last))
-            def _():
-                keep(dot(side([i_high, i_high]), pile([y_high[span, :], y_low[span, :]])))
-
-            @pl.when(last)
-            def _():
-                high, low = y_high[span, :], y_low[span, :]
-                keep(dot(side([i_high, i_high, i_low]), pile([high, low, high])))
-
-            for done in range(NB - 1):
+            factor(gram, inverse, spread_columns)
+
+            def finish(done, exact):
+                own = slice(RB * done, RB * done + RB)
+                high, low = y_high[own, :], y_low[own, :]
+                i_high, i_low = halves(inverse[...])
+                if exact:
+                    kept = dot(side([i_high, i_high, i_low]), pile([high, low, high]))
+                else:
+                    kept = dot(side([i_high, i_high]), pile([high, low]))
+                u_h, u_l = halves(kept)
+                w_high[own, :] = u_h
+                w_low[own, :] = u_l
+                if done == NB - 1:
+                    return
                 rest = slice(RB * (done + 1), D)
-                own = slice(RB * done, RB * done + RB)
-
-                def remove(change, rest=rest):
-                    left = y[rest, :] - change
-                    y[rest, :] = left
-                    high, low = halves(left)
-                    y_high[rest, :] = high
-                    y_low[rest, :] = low
-
-                @pl.when((block == done) & jnp.logical_not(last))
-                def _(rest=rest, own=own, remove=remove):
-                    u_h, u_l = w_high[own, :], w_low[own, :]
-                    l_h = dot_nt(y_high[rest, :], u_h).astype(BF16)
-                    remove(dot(side([l_h, l_h]), pile([u_h, u_l])))
-
-                @pl.when((block == done) & last)
-                def _(rest=rest, own=own, remove=remove):
-                    u_h, u_l = w_high[own, :], w_low[own, :]
+                if exact:
                     r_h, r_l = y_high[rest, :], y_low[rest, :]
                     l_h, l_l = halves(dot_nt(side([r_h, r_h, r_l]), side([u_h, u_l, u_h])))
-                    remove(dot(side([l_h, l_h, l_l]), pile([u_h, u_l, u_h])))
-
+                    change = dot(side([l_h, l_h, l_l]), pile([u_h, u_l, u_h]))
+                else:
+                    l_h = dot_nt(y_high[rest, :], u_h).astype(BF16)
+                    change = dot(side([l_h, l_h]), pile([u_h, u_l]))
+                left = y[rest, :] - change
+                high, low = halves(left)
+                y[rest, :] = left
+                y_high[rest, :] = high
+                y_low[rest, :] = low
+                high, low = high[:RB, :], low[:RB, :]
+                if exact:
+                    gram[...] = dot_nt(side([high, high, low]), side([high, low, high]))
+                else:
+                    gram[...] = dot_nt(high, high)
+
+            for done in range(NB):
+                pl.when((block == done) & jnp.logical_not(last))(
+                    functools.partial(finish, done, False)
+                )
+                pl.when((block == done) & last)(functools.partial(finish, done, True))
             return inner
 
         return lax.fori_loop(0, NB, block_step, carry)
@@ -565,6 +560,7 @@
             pltpu.VMEM((D, D), BF16),
             pltpu.VMEM((RB, RB), F32),
             pltpu.VMEM((RB, RB), F32),
+            pltpu.VMEM((RB + 8, RB), F32),
         ],
         compiler_params=params(48),
         name="sweeps",

time: 260 us -> 248 us (0.954)
  Pallas kernels: 256 us -> 244 us
    pallas_call x1, Pallas kernels: 101 us -> 89.3 us  [sweeps(): pl.pallas_call(sweeps_kernel, out_shape=[jax.ShapeDtypeStruct((D, D), BF1...]
where the time goes in v5:
time: 248 us
  Pallas kernels  244 us (98%)
  local copies, waits for them, and re-layouts  3.76 us (2%)
    pallas_call x1, Pallas kernels, sweeps(): pl.pallas_call(sweeps_kernel, out_shape=[jax.ShapeDtypeStruct((D, D), BF1...  89.3 us
    pallas_call x1, Pallas kernels, body(): pl.pallas_call(giveback_kernel, out_shape=jax.ShapeDtypeStruct((SLOTS, D)...  51.1 us
    pallas_call x1, Pallas kernels, body(): pl.pallas_call(scatter_kernel, out_shape=[jax.ShapeDtypeStruct((SLOTS, D)...  50.4 us
    pallas_call x1, Pallas kernels, body(): pl.pallas_call(reduce_kernel, out_shape=jax.ShapeDtypeStruct((PACKED, RB)...  46 us
    pallas_call x1, Pallas kernels, body(): pl.pallas_call(collect_kernel, out_shape=jax.ShapeDtypeStruct((ROWS, D),...  5.19 us

profile of v5, /device:TPU:26, one launch (start us, length us, event | category | flops | bytes accessed | tf_op | source)
XLA Modules:
  0.0 248.0 jit_solution(17241001867045870819)
XLA Ops:
  0.0 0.0 copy-start
  0.0 1.7 copy-done
  1.7 0.0 copy-start.1
  1.7 1.4 copy-done.1
  3.1 0.0 copy-start.2
  3.1 0.7 copy-done.2
  3.8 50.4 %scatter.1 = (bf16[2048,768]{1,0:T(8,128)(2,1)S(1)}, f32[128,128]{1,0:T(8,128)S(1)}, f32[768,768]{1,0:T(8,128)S(1)}, s32[1024,128]{1,0:T(8,128)S(1)}) custom-call(s32[1,1024]{1,0:T(1,128)S(1)} %bitcast.3, bf16[1024,768]{1,0:T(8,128)(2,1)S(1)} %copy-done.1, f32[768,768]{1,0:T(8,128)S(1)} %bitcast.2), custom_call_target="tpu_custom_call" | custom-call | tf_op jit(solution)/shard_map/scatter/pallas_call | solution.py:575
  54.2 2.3 moments.1.part_ref
  56.4 46.0 %reduce.1.reduced_ref = f32[2816,128]{1,0:T(8,128)S(1)} custom-call(f32[2816,128]{1,0:T(8,128)S(1)} %moments.1.part_ref), custom_call_target="tpu_custom_call" | custom-call | tf_op jit(solution)/shard_map/reduce/pallas_call | solution.py:598
  102.5 89.3 %sweeps.1 = (bf16[768,768]{1,0:T(8,128)(2,1)S(1)}, f32[8,768]{1,0:T(8,128)S(1)}) custom-call(f32[2816,128]{1,0:T(8,128)S(1)} %reduce.1.reduced_ref, f32[768,768]{1,0:T(8,128)S(1)} %get-tuple-element.13.start_ref), custom_call_target="tpu_custom_call" | custom-call | tf_op jit(solution)/shard_map/sweeps/pallas_call | solution.py:549
  191.8 51.1 %giveback.1.returned_ref = bf16[2048,768]{1,0:T(8,128)(2,1)S(1)} custom-call(bf16[2048,768]{1,0:T(8,128)(2,1)S(1)} %get-tuple-element.11.received_ref, bf16[768,768]{1,0:T(8,128)(2,1)S(1)} %get-tuple-element.14.w_ref, f32[8,768]{1,0:T(8,128)S(1)} %get-tuple-element.15.shift_ref), custom_call_target="tpu_custom_call" | custom-call | tf_op jit(solution)/shard_map/giveback/pallas_call | solution.py:613
  242.8 5.2 %collect.1 = bf16[1024,768]{1,0:T(8,128)(2,1)} custom-call(bf16[2048,768]{1,0:T(8,128)(2,1)S(1)} %giveback.1.returned_ref, s32[1024,128]{1,0:T(8,128)S(1)} %get-tuple-element.16.place_ref), custom_call_target="tpu_custom_call" | custom-call | tf_op jit(solution)/shard_map/collect/pallas_call | solution.py:622
Async XLA Ops:
  0.0 1.7 copy-start
  1.7 1.4 copy-start.1
  3.1 0.7 copy-start.2

commit v6 on v5

--- a/solution.py
+++ b/solution.py
@@ -21,6 +21,7 @@
 TN = (((0,), (0,)), ((), ()))
 VMEM = pl.BlockSpec(memory_space=pltpu.VMEM)
 ANY = pl.BlockSpec(memory_space=pl.ANY)
+HBM = pl.BlockSpec(memory_space=pltpu.HBM)
 MESH = pl.DeviceIdType.MESH
 DMA = pltpu.SemaphoreType.DMA
 PLANE = 16
@@ -71,8 +72,8 @@
 
 
 def scatter_kernel(
-    ids_ref, rows_ref, basis_ref, received_ref, got_counts_ref, got_basis_ref, place_ref,
-    buffer, counts,
+    ids_ref, rows_hbm, basis_ref, received_ref, got_counts_ref, got_basis_ref, place_ref,
+    buffer, counts, rows_ref,
     send, recv, send_count, recv_count, send_up, send_down, send_across, recv_chain, recv_across, own
 ):
     bucket, me = lax.axis_index("bucket"), lax.axis_index("replica")
@@ -83,6 +84,8 @@
     down = lax.rem(z + RING - 1, RING) * 2 + core
     across = z * 2 + (1 - core)
     peers = plane_peers(me)
+    load = pltpu.make_async_copy(rows_hbm, rows_ref, own.at[3])
+    load.start()
 
     barrier = pltpu.get_barrier_semaphore()
     for peer in peers:
@@ -132,6 +135,7 @@
         start = pl.multiple_of(cell * CAP, CAP)
         buffer[pl.ds(start, CAP), :] = dot(pick, rows_ref[...]).astype(BF16)
 
+    load.wait()
     copies = []
     for index, peer in enumerate(peers):
         fill(peer)
@@ -580,10 +584,14 @@
             jax.ShapeDtypeStruct((D, D), F32),
             jax.ShapeDtypeStruct((ROWS, 128), jnp.int32),
         ],
-        in_specs=[VMEM, VMEM, ANY],
+        in_specs=[VMEM, HBM, HBM],
         out_specs=[ANY] * 3 + [VMEM],
-        scratch_shapes=[pltpu.VMEM((SLOTS, D), BF16), pltpu.VMEM((8 * CELLS, 128), F32)]
-        + [DMA((PLANE - 1,))] * 4 + [DMA((PIECES,))] * 5 + [DMA((3,))],
+        scratch_shapes=[
+            pltpu.VMEM((SLOTS, D), BF16),
+            pltpu.VMEM((8 * CELLS, 128), F32),
+            pltpu.VMEM((ROWS, D), BF16),
+        ]
+        + [DMA((PLANE - 1,))] * 4 + [DMA((PIECES,))] * 5 + [DMA((4,))],
         compiler_params=remote(1),
         name="scatter",
     )(cell_ids.reshape(1, ROWS), rows, start_basis[0])

time: 248 us -> 248 us (level)
  no operation moved by 1% of the time
where the time goes in v6:
time: 248 us
  Pallas kernels  244 us (98%)
  local copies, waits for them, and re-layouts  3.76 us (2%)
    pallas_call x1, Pallas kernels, sweeps(): pl.pallas_call(sweeps_kernel, out_shape=[jax.ShapeDtypeStruct((D, D), BF1...  89.3 us
    pallas_call x1, Pallas kernels, body(): pl.pallas_call(giveback_kernel, out_shape=jax.ShapeDtypeStruct((SLOTS, D)...  52 us
    pallas_call x1, Pallas kernels, body(): pl.pallas_call(scatter_kernel, out_shape=[jax.ShapeDtypeStruct((SLOTS, D)...  50.6 us
    pallas_call x1, Pallas kernels, body(): pl.pallas_call(reduce_kernel, out_shape=jax.ShapeDtypeStruct((PACKED, RB)...  44.9 us
    pallas_call x1, Pallas kernels, body(): pl.pallas_call(collect_kernel, out_shape=jax.ShapeDtypeStruct((ROWS, D),...  5.19 us

profile of v6, /device:TPU:26, one launch (start us, length us, event | category | flops | bytes accessed | tf_op | source)
XLA Modules:
  0.0 248.1 jit_solution(13484753334335219165)
XLA Ops:
  0.0 0.0 copy-start
  0.0 1.7 copy-done
  1.7 0.0 copy-start.1
  1.7 1.4 copy-done.1
  3.1 0.0 copy-start.2
  3.1 0.7 copy-done.2
  3.8 50.6 %scatter.1 = (bf16[2048,768]{1,0:T(8,128)(2,1)S(1)}, f32[128,128]{1,0:T(8,128)S(1)}, f32[768,768]{1,0:T(8,128)S(1)}, s32[1024,128]{1,0:T(8,128)S(1)}) custom-call(s32[1,1024]{1,0:T(1,128)S(1)} %bitcast.3, bf16[1024,768]{1,0:T(8,128)(2,1)S(1)} %copy-done.1, f32[768,768]{1,0:T(8,128)S(1)} %bitcast.2), custom_call_target="tpu_custom_call" | custom-call | tf_op jit(solution)/shard_map/scatter/pallas_call | solution.py:579
  54.4 2.3 moments.1.part_ref
  56.6 44.9 %reduce.1.reduced_ref = f32[2816,128]{1,0:T(8,128)S(1)} custom-call(f32[2816,128]{1,0:T(8,128)S(1)} %moments.1.part_ref), custom_call_target="tpu_custom_call" | custom-call | tf_op jit(solution)/shard_map/reduce/pallas_call | solution.py:606
  101.6 89.3 %sweeps.1 = (bf16[768,768]{1,0:T(8,128)(2,1)S(1)}, f32[8,768]{1,0:T(8,128)S(1)}) custom-call(f32[2816,128]{1,0:T(8,128)S(1)} %reduce.1.reduced_ref, f32[768,768]{1,0:T(8,128)S(1)} %get-tuple-element.13.start_ref), custom_call_target="tpu_custom_call" | custom-call | tf_op jit(solution)/shard_map/sweeps/pallas_call | solution.py:553
  190.9 52.0 %giveback.1.returned_ref = bf16[2048,768]{1,0:T(8,128)(2,1)S(1)} custom-call(bf16[2048,768]{1,0:T(8,128)(2,1)S(1)} %get-tuple-element.11.received_ref, bf16[768,768]{1,0:T(8,128)(2,1)S(1)} %get-tuple-element.14.w_ref, f32[8,768]{1,0:T(8,128)S(1)} %get-tuple-element.15.shift_ref), custom_call_target="tpu_custom_call" | custom-call | tf_op jit(solution)/shard_map/giveback/pallas_call | solution.py:621
  242.9 5.2 %collect.1 = bf16[1024,768]{1,0:T(8,128)(2,1)} custom-call(bf16[2048,768]{1,0:T(8,128)(2,1)S(1)} %giveback.1.returned_ref, s32[1024,128]{1,0:T(8,128)S(1)} %get-tuple-element.16.place_ref), custom_call_target="tpu_custom_call" | custom-call | tf_op jit(solution)/shard_map/collect/pallas_call | solution.py:630
Async XLA Ops:
  0.0 1.7 copy-start
  1.7 1.4 copy-start.1
  3.1 0.7 copy-start.2
